TPU v7x, 32 devices: a whole 2x2x4 slice. The times are simulated.
32 devices in a mesh: grp: 2 (over x), rows: 16 (over z, y, core).
Axes of the slice: x: 2, y: 2, z: 4, core: 2. Of those that a mesh axis runs over, the one named last changes fastest.
Arguments:
- train_act: bfloat16 [1, 1024, 7, 7, 512], P(None, ('grp', 'rows')), parts along dimension 1, may hold values from -6 to 6
- train_grad: bfloat16 [1, 1024, 7, 7, 512], P(None, ('grp', 'rows')), parts along dimension 1, may hold values from -6 to 6
- test_act: bfloat16 [1, 32, 7, 7, 512], P(None, ('grp', 'rows')), parts along dimension 1, may hold values from -6 to 6
- test_grad: bfloat16 [1, 32, 7, 7, 512], P(None, ('grp', 'rows')), parts along dimension 1, may hold values from -6 to 6
- ckpt_weights: float32 [1], replicated, may hold values from 0.5 to 2
- owner_ids: int32 [1024, 1], P(('grp', 'rows')), parts along dimension 0, may hold values from 0 to 15; in each aligned block of 32 rows (0 to 31, 32 to 63, ...) at most 2 rows name the same one
Outputs:
- influence: float32 [1024, 16], P(('grp', 'rows')), parts along dimension 0
- owner_scores: float32 [32, 16], P(('grp', 'rows')), parts along dimension 0
There are 2 independent parts, one for each index of `grp`. A program takes and returns all parts, laid end to end along the dimension named above; an argument that names none is the same for every part. Nothing has to cross between parts.
Inputs may be any that keep to these rules, and one draw needn't show every extreme that they name: `owner_ids`: among the training examples of one device, no owner appears more than 2 times, and some owner appears exactly 2 times.
All inputs are finite; a program needn't handle non-finite values.
Results may differ from a plain program's by a relative error of at most 0.0003.
Values may be sent and summed in bfloat16 or wider, within the bound.
No kernel may reach another device: no remote copies, remote signals or barrier semaphores. Data moves between devices by JAX's collectives and lax.ppermute only.
A program may use at most 256 MiB of HBM per device.

v0:
```python
import jax
import jax.numpy as jnp
from jax import lax
from jax.sharding import PartitionSpec as P


def patch_sum(gram_raw):
    extent = gram_raw.shape[1]
    padded = jnp.pad(gram_raw, ((0, 0), (1, 1), (1, 1), (0, 0), (1, 1), (1, 1)))
    summed = jnp.zeros(gram_raw.shape, gram_raw.dtype)
    for shift_y in range(3):
        for shift_x in range(3):
            summed = (
                summed
                + padded[
                    :,
                    shift_y : shift_y + extent,
                    shift_x : shift_x + extent,
                    :,
                    shift_y : shift_y + extent,
                    shift_x : shift_x + extent,
                ]
            )
    return summed


def pair_scores(tr_act, tr_grad, te_act, te_grad):
    rows_a = tr_act.shape[0]
    extent = tr_act.shape[1]
    channels = tr_act.shape[3]
    rows_b = te_act.shape[0]
    gram_raw = jnp.dot(
        tr_act.reshape(-1, channels),
        te_act.reshape(-1, channels).T,
        preferred_element_type=jnp.float32,
    )
    gram_raw = gram_raw.reshape(rows_a, extent, extent, rows_b, extent, extent)
    grad_gram = jnp.dot(
        tr_grad.reshape(-1, channels),
        te_grad.reshape(-1, channels).T,
        preferred_element_type=jnp.float32,
    )
    grad_gram = grad_gram.reshape(rows_a, extent, extent, rows_b, extent, extent)
    kernel = patch_sum(gram_raw)
    return jnp.sum(kernel * grad_gram, axis=(1, 2, 4, 5)) / (3.0 * extent * extent * channels)


def weighted_scores(train_act, train_grad, ckpt_weights, acts, grads):
    weighted = ckpt_weights[0] * pair_scores(train_act[0], train_grad[0], acts[0], grads[0])
    return weighted


def body(train_act, train_grad, test_act, test_grad, ckpt_weights, owner_ids):
    tr_dev = train_act.shape[1]
    group_size = lax.axis_size("rows")
    weighted = weighted_scores(
        train_act,
        train_grad,
        ckpt_weights,
        lax.all_gather(test_act, "rows", axis=1, tiled=True),
        lax.all_gather(test_grad, "rows", axis=1, tiled=True),
    )
    owners = owner_ids[:, 0]
    capacity = max(2, (tr_dev + group_size - 1) // group_size)
    matched = owners[:, None] == owners[None, :]
    earlier = (
        jnp.arange(tr_dev, dtype=jnp.int32)[None, :] < jnp.arange(tr_dev, dtype=jnp.int32)[:, None]
    )
    rank_in = jnp.sum((matched & earlier).astype(jnp.int32), axis=1)
    owner_hit = owners[None, :] == jnp.arange(group_size, dtype=jnp.int32)[:, None]
    slot_hit = rank_in[None, :] == jnp.arange(capacity, dtype=jnp.int32)[:, None]
    target = (owner_hit[:, None, :] & slot_hit[None, :, :]).astype(jnp.float32)
    packed = jnp.einsum("okr,rj->okj", target, weighted, precision=lax.Precision.HIGHEST)
    received = lax.all_to_all(packed, "rows", split_axis=0, concat_axis=0, tiled=True)
    owner_total = jnp.sum(received, axis=(0, 1))[None, :]
    return (weighted, owner_total)


def solution(mesh):
    placed = (
        P(None, ("grp", "rows"), None, None, None),
        P(None, ("grp", "rows"), None, None, None),
        P(None, ("grp", "rows"), None, None, None),
        P(None, ("grp", "rows"), None, None, None),
        P(),
        P(("grp", "rows"), None),
    )
    return jax.shard_map(
        body,
        mesh=mesh,
        in_specs=placed,
        out_specs=(P(("grp", "rows"), None), P(("grp", "rows"), None)),
        check_vma=False,
    )
```

profile of v0, /device:TPU:0, one launch (start us, length us, event | category | flops | bytes accessed | tf_op | source)
XLA Modules:
  0.0 109.8 jit_solution(8960686975599864471)
XLA Ops:
  0.6 0.0 copy-start
  0.6 0.0 copy-start.2
  0.7 0.8 iota_compare_fusion.1
  1.5 1.0 convert_reduce_fusion
  2.5 26.1 %all_gather.6 = bf16[1,16,7,7,512]{4,3,2,0,1:T(8,128)(2,1)S(1)} all-gather(bf16[1,1,7,7,512]{4,3,2,0,1:T(8,128)(2,1)} %bitcast.36), channel_id=1, replica_groups=mesh['grp'=2,'rows'=16] {'rows'}, dimensions={1}, use_global_device_ids=true | all-gather | bytes 852992 | tf_op jit(solution)/shard_map/all_gather | solution.py:60
  28.6 20.3 %all_gather.7 = bf16[1,16,7,7,512]{4,3,2,0,1:T(8,128)(2,1)S(1)} all-gather(bf16[1,1,7,7,512]{4,3,2,0,1:T(8,128)(2,1)} %bitcast.37), channel_id=1, replica_groups=mesh['grp'=2,'rows'=16] {'rows'}, dimensions={1}, use_global_device_ids=true | all-gather | bytes 852992 | tf_op jit(solution)/shard_map/all_gather | solution.py:61
  49.5 0.0 copy-done
  49.5 9.6 %fusion.11 = f32[32,7,7,16,7,7]{0,3,5,4,2,1:T(8,128)} fusion(bf16[1,32,7,7,512]{4,1,3,2,0:T(8,128)(2,1)S(1)} %copy-done, bf16[1,16,7,7,512]{4,3,2,0,1:T(8,128)(2,1)S(1)} %all_gather.6), kind=kOutput, calls=%fused_computation.19 | convolution fusion | flops 1258815488 | bytes 7325696 | tf_op jit(solution)/shard_map/dot_general | solution.py:32
  59.1 0.0 copy-done.2
  59.1 40.5 %fusion.9 = f32[32,16]{0,1:T(8,128)S(1)} fusion(f32[32,7,7,16,7,7]{0,3,5,4,2,1:T(8,128)} %fusion.11, bf16[1,32,7,7,512]{4,1,3,2,0:T(8,128)(2,1)S(1)} %copy-done.2, bf16[1,16,7,7,512]{4,3,2,0,1:T(8,128)(2,1)S(1)} %all_gather.7), kind=kOutput, calls=%fused_computation.17 | convolution fusion | flops 1271108096 | bytes 7327744 | tf_op jit(solution)/shard_map/dot_general | solution.py:38
  99.7 0.0 copy-start.1
  99.7 0.1 fusion.18
  99.8 9.4 %all_to_all.5 = f32[16,2,16]{2,1,0:T(2,128)S(1)} all-to-all(f32[16,2,16]{2,1,0:T(2,128)S(1)} %copy.19), channel_id=1, replica_groups=mesh['grp'=2,'rows'=16] {'rows'}, dimensions={0} | all-to-all | bytes 4096 | tf_op jit(solution)/shard_map/all_to_all | solution.py:74
  109.3 0.5 reduce_sum.29
  109.8 0.0 copy-done.1
  (3 shorter events, 0.0 us)
Async XLA Ops:
  0.6 48.9 %copy-start = (bf16[1,32,7,7,512]{4,1,3,2,0:T(8,128)(2,1)S(1)}, bf16[1,32,7,7,512]{4,1,3,2,0:T(8,128)(2,1)}, u32[]{:S(2)}) copy-start(bf16[1,32,7,7,512]{4,1,3,2,0:T(8,128)(2,1)} %param.6) | copy-start | bytes 4816900
  0.6 58.5 %copy-start.2 = (bf16[1,32,7,7,512]{4,1,3,2,0:T(8,128)(2,1)S(1)}, bf16[1,32,7,7,512]{4,1,3,2,0:T(8,128)(2,1)}, u32[]{:S(2)}) copy-start(bf16[1,32,7,7,512]{4,1,3,2,0:T(8,128)(2,1)} %param.7) | copy-start | bytes 4816900
  99.7 10.2 %copy-start.1 = (f32[32,16]{0,1:T(8,128)}, f32[32,16]{0,1:T(8,128)S(1)}, u32[]{:S(2)}) copy-start(f32[32,16]{0,1:T(8,128)S(1)} %broadcast_multiply_fusion) | copy-start | bytes 6148
where the time goes:
time: 110 us
  blocking collectives  55.8 us (51%)
  matrix products  50.2 us (46%)
  other arithmetic  2.37 us (2%)
  between operations  1.35 us (1%)
    dot_general x1, matrix products, pair_scores(): jnp.dot(tr_grad.reshape(-1, channels), te_grad.reshape(-1, channels).T, p...  40.5 us
    all_gather x1, blocking collectives, body(): lax.all_gather(test_act, 'rows', axis=1, tiled=True)  26.1 us
    all_gather x1, blocking collectives, body(): lax.all_gather(test_grad, 'rows', axis=1, tiled=True)  20.3 us
    dot_general x1, matrix products, pair_scores(): jnp.dot(tr_act.reshape(-1, channels), te_act.reshape(-1, channels).T, pre...  9.56 us
    all_to_all x1, blocking collectives, body(): lax.all_to_all(packed, 'rows', split_axis=0, concat_axis=0, tiled=True)  9.44 us

commit v1 on v0

v1 whole, which is shorter than its diff:
```python
import functools

import jax
import jax.numpy as jnp
from jax import lax
from jax.experimental import pallas as pl
from jax.experimental.pallas import tpu as pltpu
from jax.sharding import PartitionSpec as P

CHUNK = 4
LANES = 64
HIGHEST = lax.Precision.HIGHEST


def nt_dot(a, b, precision=None):
    return lax.dot_general(
        a, b, (((1,), (1,)), ((), ())), precision=precision, preferred_element_type=jnp.float32
    )


def pack_test(act, grad):
    side, channels = act.shape[0], act.shape[2]
    act = jnp.pad(act, ((0, 0), (0, 8 - side), (0, 0)))
    grad = jnp.pad(grad, ((0, 0), (0, 8 - side), (0, 0)))
    pieces = (act[: side - 1], grad[: side - 1], act[side - 1 :], grad[side - 1 :])
    return jnp.concatenate([piece.reshape(-1, channels) for piece in pieces], axis=0)


def chunk_kernel(base, last, side, scale, chip_ref, weight_ref, ids_ref, prev_ref, *refs):
    tests = refs[:CHUNK]
    train_act = refs[CHUNK : CHUNK + 2]
    train_grad = refs[CHUNK + 2 : CHUNK + 4]
    outs = refs[CHUNK + 4 : CHUNK + 6 if last else CHUNK + 5]
    act_w, grad_w, raw, gram = refs[-4:]
    head = (side - 1) * 8
    channels = act_w.shape[1]
    for t in range(CHUNK):
        act_w[t * LANES : t * LANES + head] = tests[t][:head]
        grad_w[t * LANES : t * LANES + head] = tests[t][head : 2 * head]
        tail = tests[t][2 * head : 2 * head + 16].astype(jnp.float32)
        blank = jnp.zeros((8, channels), jnp.float32)
        act_w[t * LANES + head : (t + 1) * LANES] = jnp.concatenate([tail[:8], blank]).astype(
            jnp.bfloat16
        )
        grad_w[t * LANES + head : (t + 1) * LANES] = jnp.concatenate([tail[8:], blank]).astype(
            jnp.bfloat16
        )

    chips = prev_ref.shape[1]
    rows = train_act[0].shape[0] // (side * side)
    line = side * rows
    lanes = CHUNK * LANES
    tested = lax.broadcasted_iota(jnp.int32, (chips, lanes), 0) ^ chip_ref[0]
    holds = lax.broadcasted_iota(jnp.int32, (chips, lanes), 1) // LANES + base
    chosen = (tested == holds).astype(jnp.float32)

    scores = []
    for half in range(2):
        for a in range(side):
            cut = slice(a * line, (a + 1) * line)
            raw[half, cut] = nt_dot(train_act[half][cut], act_w[...])
            gram[half, cut] = nt_dot(train_grad[half][cut], grad_w[...])
        totals = []
        for lane in range(0, lanes, 128):
            total = jnp.zeros((rows, 128), jnp.float32)
            for a in range(side):
                columns = []
                for b in range(side):
                    at = (a * side + b) * rows
                    column = raw[half, at : at + rows, lane : lane + 128]
                    if a > 0:
                        column += pltpu.roll(
                            raw[half, at - line : at - line + rows, lane : lane + 128], 8, 1
                        )
                    if a < side - 1:
                        column += pltpu.roll(
                            raw[half, at + line : at + line + rows, lane : lane + 128], 120, 1
                        )
                    columns.append(column)
                for b in range(side):
                    at = (a * side + b) * rows
                    patch = columns[b]
                    if b > 0:
                        patch += pltpu.roll(columns[b - 1], 1, 1)
                    if b < side - 1:
                        patch += pltpu.roll(columns[b + 1], 127, 1)
                    total += patch * gram[half, at : at + rows, lane : lane + 128]
            totals.append(total)
        scores.append(nt_dot(chosen, jnp.concatenate(totals, axis=1), HIGHEST) + prev_ref[half])
    if not last:
        for half in range(2):
            outs[0][half] = scores[half]
        return
    owned = 0.0
    for half in range(2):
        influence = scores[half] * (weight_ref[0] * scale)
        outs[0][half] = influence
        number_of = outs[1].shape[0]
        owner = lax.broadcasted_iota(jnp.int32, (number_of, rows), 0)
        hit = (owner == ids_ref[half : half + 1]).astype(jnp.float32)
        owned += nt_dot(hit, influence, HIGHEST)
    outs[1][...] = owned


def chunk_scores(base, last, side, owners, scale, chip, weight, ids, prev, tests, acts, grads):
    rows, channels = acts[0].shape
    lanes = CHUNK * LANES
    out_shape = [jax.ShapeDtypeStruct(prev.shape, jnp.float32)]
    if last:
        out_shape.append(jax.ShapeDtypeStruct((owners, prev.shape[1]), jnp.float32))
    vmem, smem = pl.BlockSpec(memory_space=pltpu.VMEM), pl.BlockSpec(memory_space=pltpu.SMEM)
    return pl.pallas_call(
        functools.partial(chunk_kernel, base, last, side, scale),
        out_shape=out_shape,
        in_specs=[smem, smem] + [vmem] * (2 + CHUNK + 4),
        out_specs=[vmem] * len(out_shape),
        scratch_shapes=[
            pltpu.VMEM((lanes, channels), jnp.bfloat16),
            pltpu.VMEM((lanes, channels), jnp.bfloat16),
            pltpu.VMEM((2, rows, lanes), jnp.float32),
            pltpu.VMEM((2, rows, lanes), jnp.float32),
        ],
        compiler_params=pltpu.CompilerParams(vmem_limit_bytes=48 * 1024 * 1024),
        cost_estimate=pl.CostEstimate(
            flops=8 * rows * lanes * channels, bytes_accessed=8 * rows * channels, transcendentals=0
        ),
        name="chunk_scores",
    )(chip, weight, ids, prev, *tests, *acts, *grads)


def across(x, distance):
    size = lax.axis_size("rows")
    return lax.ppermute(x, "rows", [(i, i ^ distance) for i in range(size)])


def gather_tests(own):
    chips = lax.axis_size("rows") // 2
    held = {0: own}
    if chips == 8:
        held[4] = across(own, 8)
        held[6] = across(own, 12)
        held[2] = across(own, 4)
        held[1] = across(own, 2)
        held[3] = across(own, 6)
        held[5] = across(held[4], 2)
        held[7] = across(held[6], 2)
        return held
    bit = 1
    while bit < chips:
        for known in list(held):
            held[known ^ bit] = across(held[known], 2 * bit)
        bit *= 2
    return held


def body(train_act, train_grad, test_act, test_grad, ckpt_weights, owner_ids):
    tr_dev, side, channels = train_act.shape[1], train_act.shape[2], train_act.shape[4]
    size = lax.axis_size("rows")
    chips = size // 2
    me = lax.axis_index("rows")
    held = gather_tests(pack_test(test_act[0, 0], test_grad[0, 0]))

    own_act = train_act[0].transpose(1, 2, 0, 3).reshape(-1, channels)
    own_grad = train_grad[0].transpose(1, 2, 0, 3).reshape(-1, channels)
    acts = (own_act, across(own_act, 1))
    grads = (own_grad, across(own_grad, 1))
    own_ids = owner_ids.reshape(1, tr_dev)
    ids = jnp.concatenate([own_ids, across(own_ids, 1)], axis=0)

    chip = (me // 2).reshape(1)
    scale = 1.0 / (3.0 * side * side * channels)
    scores = jnp.zeros((2, chips, tr_dev), jnp.float32)
    for base in range(0, chips, CHUNK):
        last = base + CHUNK >= chips
        tests = [held[base + t] for t in range(CHUNK)]
        done = chunk_scores(
            base, last, side, size, scale, chip, ckpt_weights, ids, scores, tests, acts, grads
        )
        scores = done[0]
    mine, packed = scores[0], done[1]

    other = across(scores[1], 1)
    received = lax.all_to_all(packed, "rows", split_axis=0, concat_axis=0, tiled=True)
    core = lax.broadcasted_iota(jnp.int32, (1, 2, 1), 1)
    influence = jnp.where(core == me % 2, mine[:, None, :], other[:, None, :]).reshape(size, tr_dev)
    totals = jnp.sum(received.reshape(chips, 2, chips), axis=0)
    return influence.T, totals.T.reshape(1, size)


def solution(mesh):
    placed = (
        P(None, ("grp", "rows"), None, None, None),
        P(None, ("grp", "rows"), None, None, None),
        P(None, ("grp", "rows"), None, None, None),
        P(None, ("grp", "rows"), None, None, None),
        P(),
        P(("grp", "rows"), None),
    )
    return jax.shard_map(
        body,
        mesh=mesh,
        in_specs=placed,
        out_specs=(P(("grp", "rows"), None), P(("grp", "rows"), None)),
        check_vma=False,
    )
```

time: 110 us -> 49.3 us (0.45)
  blocking collectives: 55.8 us -> 0 us
  matrix products: 50.2 us -> 0 us
  starting transfers between devices: 0 us -> 17.1 us
  waiting for transfers between devices: 0 us -> 12.8 us
  Pallas kernels: 0 us -> 11.1 us
  local copies, waits for them, and re-layouts: 0.05 us -> 5.21 us
    dot_general x3 -> x0, matrix products: 50.2 us -> none  [the longest x1 40.5 us: pair_scores(): jnp.dot(tr_grad.reshape(-1, channels), te_grad.reshape(-1, channels).T, p...]
    all_gather x2 -> x0, blocking collectives: 46.4 us -> none  [the longest x1 26.1 us: body(): lax.all_gather(test_act, 'rows', axis=1, tiled=True)]
    ppermute x0 -> x11, starting transfers between devices: none -> 12.1 us  [across(): return lax.ppermute(x, 'rows', [(i, i ^ distance) for i in range(size)])]
    pallas_call x0 -> x2, Pallas kernels: none -> 11.1 us  [chunk_scores(): pl.pallas_call(functools.partial(chunk_kernel, base, last, side, scale),...]
    all_to_all x1 -> x0, blocking collectives: 9.44 us -> none  [body(): lax.all_to_all(packed, 'rows', split_axis=0, concat_axis=0, tiled=True)]
    ppermute x0 -> x11, waiting for transfers between devices: none -> 6.58 us  [across(): return lax.ppermute(x, 'rows', [(i, i ^ distance) for i in range(size)])]
    all_to_all x0 -> x1, waiting for transfers between devices: none -> 6.22 us  [body(): lax.all_to_all(packed, 'rows', split_axis=0, concat_axis=0, tiled=True)]
    all_to_all x0 -> x1, starting transfers between devices: none -> 4.99 us  [body(): lax.all_to_all(packed, 'rows', split_axis=0, concat_axis=0, tiled=True)]
  transfers between devices with their start and end apart: 0 -> 12, of which waited for: 0 -> 3; matrix products, arithmetic and copies ran while one was open for 0% -> 6% of each run, Pallas kernels for 0% -> 11%
where the time goes in v1:
time: 49.3 us; the launch traced here: 48.9 us
  starting transfers between devices  17.1 us (35%)
  waiting for transfers between devices  12.8 us (26%)
  Pallas kernels  11.1 us (23%)
  local copies, waits for them, and re-layouts  5.21 us (11%)
  between operations  1.38 us (3%)
  other arithmetic  1.37 us (3%)
    ppermute x11, starting transfers between devices, across(): return lax.ppermute(x, 'rows', [(i, i ^ distance) for i in range(size)])  12.1 us
    pallas_call x2, Pallas kernels, chunk_scores(): pl.pallas_call(functools.partial(chunk_kernel, base, last, side, scale),...  11.1 us
    ppermute x11, waiting for transfers between devices, across(): return lax.ppermute(x, 'rows', [(i, i ^ distance) for i in range(size)])  6.58 us
    all_to_all x1, waiting for transfers between devices, body(): lax.all_to_all(packed, 'rows', split_axis=0, concat_axis=0, tiled=True)  6.22 us
    all_to_all x1, starting transfers between devices, body(): lax.all_to_all(packed, 'rows', split_axis=0, concat_axis=0, tiled=True)  4.99 us
    unnamed x8, local copies, waits for them, and re-layouts  2.86 us
    reshape x2, local copies, waits for them, and re-layouts, pack_test(): piece.reshape(-1, channels)  1.56 us
  transfers between devices with their start and end apart: 12, of which 3 were waited for; matrix products, arithmetic and copies ran while one was open for 6% of the time, Pallas kernels for 11%

profile of v1, /device:TPU:0, one launch (start us, length us, event | category | flops | bytes accessed | tf_op | source)
XLA Modules:
  0.0 48.9 jit_solution(7822606151154432288)
XLA Ops:
  0.6 0.5 %collective-permute-start.4 = (bf16[1568,512]{1,0:T(8,128)(2,1)}, bf16[1568,512]{1,0:T(8,128)(2,1)S(1)}, u32[]{:S(2)}, u32[]{:S(2)}) collective-permute-start(bf16[1568,512]{1,0:T(8,128)(2,1)} %bitcast.35), channel_id=1, source_target_pairs={{0,1},{1,0},{2,3},{3,2},{4,5},{5,4},{6,7},{7,6},{8,9},{9,8},{10,11... | collective-permute-start | bytes 4816904 | tf_op jit(solution)/shard_map/ppermute | solution.py:133
  1.1 0.1 collective-permute-start.5
  1.2 0.7 %fusion.2 = (bf16[8,512]{1,0:T(8,128)(2,1)S(1)}, bf16[8,512]{1,0:T(8,128)(2,1)S(1)}) fusion(bf16[7,7,512]{2,1,0:T(8,128)(2,1)} %bitcast.41, bf16[7,7,512]{2,1,0:T(8,128)(2,1)} %bitcast.43), kind=kLoop, calls=%fused_computation.7 | loop fusion | bytes 116736 | tf_op jit(solution)/shard_map/reshape | solution.py:26
  1.9 0.8 %fusion = (bf16[48,512]{1,0:T(8,128)(2,1)S(1)}, bf16[48,512]{1,0:T(8,128)(2,1)S(1)}) fusion(bf16[7,7,512]{2,1,0:T(8,128)(2,1)} %bitcast.42, bf16[7,7,512]{2,1,0:T(8,128)(2,1)} %bitcast.44), kind=kLoop, calls=%fused_computation.5 | loop fusion | bytes 198656 | tf_op jit(solution)/shard_map/reshape | solution.py:26
  2.8 3.0 %collective-permute-start.1 = (bf16[112,512]{1,0:T(8,128)(2,1)S(1)}, bf16[112,512]{1,0:T(8,128)(2,1)S(1)}, u32[]{:S(2)}, u32[]{:S(2)}) collective-permute-start(bf16[112,512]{1,0:T(8,128)(2,1)S(1)} %pad_maximum_fusion.refs_0_), channel_id=1, source_target_pairs={{0,2},{1,3},{2,0},{3,1},{4,6},{5,7},{6,4},{7,5},{8,10},{9,11},{10,... | collective-permute-start | bytes 344072 | tf_op jit(solution)/shard_map/ppermute | solution.py:133
  5.8 1.6 %collective-permute-start.2 = (bf16[112,512]{1,0:T(8,128)(2,1)S(1)}, bf16[112,512]{1,0:T(8,128)(2,1)S(1)}, u32[]{:S(2)}, u32[]{:S(2)}) collective-permute-start(bf16[112,512]{1,0:T(8,128)(2,1)S(1)} %pad_maximum_fusion.refs_0_), channel_id=1, source_target_pairs={{0,4},{1,5},{2,6},{3,7},{4,0},{5,1},{6,2},{7,3},{8,12},{9,13},{10,... | collective-permute-start | bytes 344072 | tf_op jit(solution)/shard_map/ppermute | solution.py:133
  7.4 1.3 %collective-permute-done = s32[1,32]{1,0:T(1,128)S(1)} collective-permute-done((s32[1,32]{1,0:T(1,128)}, s32[1,32]{1,0:T(1,128)S(1)}, u32[]{:S(2)}, u32[]{:S(2)}) %collective-permute-start) | collective-permute-done | bytes 160 | tf_op jit(solution)/shard_map/ppermute | solution.py:133
  8.7 2.6 %collective-permute-start.6 = (bf16[112,512]{1,0:T(8,128)(2,1)S(1)}, bf16[112,512]{1,0:T(8,128)(2,1)S(1)}, u32[]{:S(2)}, u32[]{:S(2)}) collective-permute-start(bf16[112,512]{1,0:T(8,128)(2,1)S(1)} %pad_maximum_fusion.refs_0_), channel_id=1, source_target_pairs={{0,8},{1,9},{2,10},{3,11},{4,12},{5,13},{6,14},{7,15},{8,0},{9,1},... | collective-permute-start | bytes 344072 | tf_op jit(solution)/shard_map/ppermute | solution.py:133
  11.2 1.8 %collective-permute-start.8 = (bf16[112,512]{1,0:T(8,128)(2,1)S(1)}, bf16[112,512]{1,0:T(8,128)(2,1)S(1)}, u32[]{:S(2)}, u32[]{:S(2)}) collective-permute-start(bf16[112,512]{1,0:T(8,128)(2,1)S(1)} %pad_maximum_fusion.refs_0_), channel_id=1, source_target_pairs={{0,12},{1,13},{2,14},{3,15},{4,8},{5,9},{6,10},{7,11},{8,4},{9,5},... | collective-permute-start | bytes 344072 | tf_op jit(solution)/shard_map/ppermute | solution.py:133
  13.0 0.5 %collective-permute-start.3 = (bf16[112,512]{1,0:T(8,128)(2,1)S(1)}, bf16[112,512]{1,0:T(8,128)(2,1)S(1)}, u32[]{:S(2)}, u32[]{:S(2)}) collective-permute-start(bf16[112,512]{1,0:T(8,128)(2,1)S(1)} %pad_maximum_fusion.refs_0_), channel_id=1, source_target_pairs={{0,6},{1,7},{2,4},{3,5},{4,2},{5,3},{6,0},{7,1},{8,14},{9,15},{10,... | collective-permute-start | bytes 344072 | tf_op jit(solution)/shard_map/ppermute | solution.py:133
  14.2 0.7 %pad_add_fusion.ids_ref = s32[2,32]{1,0:T(2,128)S(1)} fusion(s32[1,32]{1,0:T(1,128)S(1)} %collective-permute-done, s32[1,32]{1,0:T(1,128)} %bitcast.50), kind=kLoop, calls=%fused_computation.12 | loop fusion | flops 64 | bytes 512 | tf_op jit(solution)/shard_map/concatenate | solution.py:168
  14.9 5.3 %collective-permute-done.6.refs_0_ = bf16[112,512]{1,0:T(8,128)(2,1)S(1)} collective-permute-done((bf16[112,512]{1,0:T(8,128)(2,1)S(1)}, bf16[112,512]{1,0:T(8,128)(2,1)S(1)}, u32[]{:S(2)}, u32[]{:S(2)}) %collective-permute-start.6) | collective-permute-done | bytes 114720 | tf_op jit(solution)/shard_map/ppermute | solution.py:133
  20.2 1.2 %collective-permute-start.7 = (bf16[112,512]{1,0:T(8,128)(2,1)S(1)}, bf16[112,512]{1,0:T(8,128)(2,1)S(1)}, u32[]{:S(2)}, u32[]{:S(2)}) collective-permute-start(bf16[112,512]{1,0:T(8,128)(2,1)S(1)} %collective-permute-done.6.refs_0_), channel_id=1, source_target_pairs={{0,2},{1,3},{2,0},{3,1},{4,6},{5,7},{6,4},{7,5},{8,10},{9,11},{10,... | collective-permute-start | bytes 344072 | tf_op jit(solution)/shard_map/ppermute | solution.py:133
  21.4 0.8 %collective-permute-start.9 = (bf16[112,512]{1,0:T(8,128)(2,1)S(1)}, bf16[112,512]{1,0:T(8,128)(2,1)S(1)}, u32[]{:S(2)}, u32[]{:S(2)}) collective-permute-start(bf16[112,512]{1,0:T(8,128)(2,1)S(1)} %collective-permute-done.8.refs_2_), channel_id=1, source_target_pairs={{0,2},{1,3},{2,0},{3,1},{4,6},{5,7},{6,4},{7,5},{8,10},{9,11},{10,... | collective-permute-start | bytes 344072 | tf_op jit(solution)/shard_map/ppermute | solution.py:133
  22.2 1.4 %copy-done = bf16[1,32,7,7,512]{4,1,3,2,0:T(8,128)(2,1)S(1)} copy-done((bf16[1,32,7,7,512]{4,1,3,2,0:T(8,128)(2,1)S(1)}, bf16[1,32,7,7,512]{4,1,3,2,0:T(8,128)(2,1)}, u32[]{:S(2)}) %copy-start) | copy-done | bytes 1605656
  23.7 1.4 %copy-done.2 = bf16[1,32,7,7,512]{4,1,3,2,0:T(8,128)(2,1)S(1)} copy-done((bf16[1,32,7,7,512]{4,1,3,2,0:T(8,128)(2,1)S(1)}, bf16[1,32,7,7,512]{4,1,3,2,0:T(8,128)(2,1)}, u32[]{:S(2)}) %copy-start.2) | copy-done | bytes 1605656
  25.1 5.3 %chunk_scores.2.prev_ref = f32[2,8,32]{2,1,0:T(8,128)S(1)} custom-call(s32[1]{0:T(128)} %bitcast.chip_ref, f32[1]{0:T(128)S(6)} %copy.17.weight_ref, s32[2,32]{1,0:T(2,128)S(1)} %pad_add_fusion.ids_ref, f32[2,8,32]{2,1,0:T(8,128)S(1)} %broadcast_in_dim.41.prev_ref, bf16[112,512]{1,0:T(8,128)(2,1)S(1)} %pad_maximum_fusion.refs_0_, ...), custom_call_target="tpu_custom_call" | custom-call | flops 1644167168 | bytes 6422528 | tf_op jit(solution)/shard_map/chunk_scores/pallas_call | solution.py:112
  30.4 5.8 %chunk_scores.3 = (f32[2,8,32]{2,1,0:T(8,128)S(1)}, f32[16,8]{1,0:T(8,128)}) custom-call(s32[1]{0:T(128)} %bitcast.chip_ref, f32[1]{0:T(128)S(6)} %copy.17.weight_ref, s32[2,32]{1,0:T(2,128)S(1)} %pad_add_fusion.ids_ref, f32[2,8,32]{2,1,0:T(8,128)S(1)} %chunk_scores.2.prev_ref, bf16[112,512]{1,0:T(8,128)(2,1)S(1)} %collective-permute-done.6.refs_0_, ...), custom_call_target="tpu_custom_call" | custom-call | flops 1644167168 | bytes 6422528 | tf_op jit(solution)/shard_map/chunk_scores/pallas_call | solution.py:112
  36.2 5.0 %all-to-all-start = ((f32[16,1,8]{2,1,0:T(1,128)}), f32[16,1,8]{2,1,0:T(1,128)S(1)}, u32[]{:S(2)}, u32[]{:S(2)}) async-start(f32[16,1,8]{2,1,0:T(1,128)} %bitcast.26), calls=%async_computation | async-start | bytes 16384 | tf_op jit(solution)/shard_map/all_to_all | solution.py:183
  41.2 0.1 broadcast_in_dim.39
  41.3 6.2 %all-to-all-done = f32[16,1,8]{2,1,0:T(1,128)S(1)} async-done(((f32[16,1,8]{2,1,0:T(1,128)}), f32[16,1,8]{2,1,0:T(1,128)S(1)}, u32[]{:S(2)}, u32[]{:S(2)}) %all-to-all-start) | async-done | bytes 544 | tf_op jit(solution)/shard_map/all_to_all | solution.py:183
  47.6 0.1 copy.14
  47.7 0.6 %reshape.57 = f32[1,16]{1,0:T(1,128)} reshape(f32[8,2]{1,0:T(8,128)S(1)} %copy.14) | data formatting | bytes 128 | tf_op jit(solution)/shard_map/reshape | solution.py:187
  48.3 0.7 %select_bitcast_fusion = f32[32,16]{0,1:T(8,128)} fusion(f32[16,32]{1,0:T(8,128)S(1)} %bitcast.46, f32[16,32]{1,0:T(8,128)S(1)} %bitcast.45, pred[16]{0:T(512)(128)(4,1)S(1)} %broadcast_in_dim.39), kind=kLoop, calls=%fused_computation.9 | loop fusion | flops 512 | bytes 6160 | tf_op jit(solution)/shard_map/transpose | solution.py:187
  (25 shorter events, 0.1 us)
Async XLA Ops:
  0.6 21.6 %collective-permute-start.4 = (bf16[1568,512]{1,0:T(8,128)(2,1)}, bf16[1568,512]{1,0:T(8,128)(2,1)S(1)}, u32[]{:S(2)}, u32[]{:S(2)}) collective-permute-start(bf16[1568,512]{1,0:T(8,128)(2,1)} %bitcast.35), channel_id=1, source_target_pairs={{0,1},{1,0},{2,3},{3,2},{4,5},{5,4},{6,7},{7,6},{8,9},{9,8},{10,11... | collective-permute-start | bytes 4816904 | tf_op jit(solution)/shard_map/ppermute | solution.py:133
  1.1 21.1 %collective-permute-start.5 = (bf16[1568,512]{1,0:T(8,128)(2,1)}, bf16[1568,512]{1,0:T(8,128)(2,1)}, u32[]{:S(2)}, u32[]{:S(2)}) collective-permute-start(bf16[1568,512]{1,0:T(8,128)(2,1)} %bitcast.38), channel_id=1, source_target_pairs={{0,1},{1,0},{2,3},{3,2},{4,5},{5,4},{6,7},{7,6},{8,9},{9,8},{10,11... | collective-permute-start | bytes 4816904 | tf_op jit(solution)/shard_map/ppermute | solution.py:133
  2.8 8.4 %collective-permute-start.1 = (bf16[112,512]{1,0:T(8,128)(2,1)S(1)}, bf16[112,512]{1,0:T(8,128)(2,1)S(1)}, u32[]{:S(2)}, u32[]{:S(2)}) collective-permute-start(bf16[112,512]{1,0:T(8,128)(2,1)S(1)} %pad_maximum_fusion.refs_0_), channel_id=1, source_target_pairs={{0,2},{1,3},{2,0},{3,1},{4,6},{5,7},{6,4},{7,5},{8,10},{9,11},{10,... | collective-permute-start | bytes 344072 | tf_op jit(solution)/shard_map/ppermute | solution.py:133
  5.8 7.2 %collective-permute-start.2 = (bf16[112,512]{1,0:T(8,128)(2,1)S(1)}, bf16[112,512]{1,0:T(8,128)(2,1)S(1)}, u32[]{:S(2)}, u32[]{:S(2)}) collective-permute-start(bf16[112,512]{1,0:T(8,128)(2,1)S(1)} %pad_maximum_fusion.refs_0_), channel_id=1, source_target_pairs={{0,4},{1,5},{2,6},{3,7},{4,0},{5,1},{6,2},{7,3},{8,12},{9,13},{10,... | collective-permute-start | bytes 344072 | tf_op jit(solution)/shard_map/ppermute | solution.py:133
  7.4 1.3 %collective-permute-start = (s32[1,32]{1,0:T(1,128)}, s32[1,32]{1,0:T(1,128)S(1)}, u32[]{:S(2)}, u32[]{:S(2)}) collective-permute-start(s32[1,32]{1,0:T(1,128)} %bitcast.49), channel_id=1, source_target_pairs={{0,1},{1,0},{2,3},{3,2},{4,5},{5,4},{6,7},{7,6},{8,9},{9,8},{10,11... | collective-permute-start | bytes 392 | tf_op jit(solution)/shard_map/ppermute | solution.py:133
  8.7 11.5 %collective-permute-start.6 = (bf16[112,512]{1,0:T(8,128)(2,1)S(1)}, bf16[112,512]{1,0:T(8,128)(2,1)S(1)}, u32[]{:S(2)}, u32[]{:S(2)}) collective-permute-start(bf16[112,512]{1,0:T(8,128)(2,1)S(1)} %pad_maximum_fusion.refs_0_), channel_id=1, source_target_pairs={{0,8},{1,9},{2,10},{3,11},{4,12},{5,13},{6,14},{7,15},{8,0},{9,1},... | collective-permute-start | bytes 344072 | tf_op jit(solution)/shard_map/ppermute | solution.py:133
  11.2 10.1 %collective-permute-start.8 = (bf16[112,512]{1,0:T(8,128)(2,1)S(1)}, bf16[112,512]{1,0:T(8,128)(2,1)S(1)}, u32[]{:S(2)}, u32[]{:S(2)}) collective-permute-start(bf16[112,512]{1,0:T(8,128)(2,1)S(1)} %pad_maximum_fusion.refs_0_), channel_id=1, source_target_pairs={{0,12},{1,13},{2,14},{3,15},{4,8},{5,9},{6,10},{7,11},{8,4},{9,5},... | collective-permute-start | bytes 344072 | tf_op jit(solution)/shard_map/ppermute | solution.py:133
  13.0 9.2 %collective-permute-start.3 = (bf16[112,512]{1,0:T(8,128)(2,1)S(1)}, bf16[112,512]{1,0:T(8,128)(2,1)S(1)}, u32[]{:S(2)}, u32[]{:S(2)}) collective-permute-start(bf16[112,512]{1,0:T(8,128)(2,1)S(1)} %pad_maximum_fusion.refs_0_), channel_id=1, source_target_pairs={{0,6},{1,7},{2,4},{3,5},{4,2},{5,3},{6,0},{7,1},{8,14},{9,15},{10,... | collective-permute-start | bytes 344072 | tf_op jit(solution)/shard_map/ppermute | solution.py:133
  20.2 10.2 %collective-permute-start.7 = (bf16[112,512]{1,0:T(8,128)(2,1)S(1)}, bf16[112,512]{1,0:T(8,128)(2,1)S(1)}, u32[]{:S(2)}, u32[]{:S(2)}) collective-permute-start(bf16[112,512]{1,0:T(8,128)(2,1)S(1)} %collective-permute-done.6.refs_0_), channel_id=1, source_target_pairs={{0,2},{1,3},{2,0},{3,1},{4,6},{5,7},{6,4},{7,5},{8,10},{9,11},{10,... | collective-permute-start | bytes 344072 | tf_op jit(solution)/shard_map/ppermute | solution.py:133
  21.4 9.0 %collective-permute-start.9 = (bf16[112,512]{1,0:T(8,128)(2,1)S(1)}, bf16[112,512]{1,0:T(8,128)(2,1)S(1)}, u32[]{:S(2)}, u32[]{:S(2)}) collective-permute-start(bf16[112,512]{1,0:T(8,128)(2,1)S(1)} %collective-permute-done.8.refs_2_), channel_id=1, source_target_pairs={{0,2},{1,3},{2,0},{3,1},{4,6},{5,7},{6,4},{7,5},{8,10},{9,11},{10,... | collective-permute-start | bytes 344072 | tf_op jit(solution)/shard_map/ppermute | solution.py:133
  22.2 1.4 %copy-start = (bf16[1,32,7,7,512]{4,1,3,2,0:T(8,128)(2,1)S(1)}, bf16[1,32,7,7,512]{4,1,3,2,0:T(8,128)(2,1)}, u32[]{:S(2)}) copy-start(bf16[1,32,7,7,512]{4,1,3,2,0:T(8,128)(2,1)} %param.6) | copy-start | bytes 4816900
  23.7 1.4 %copy-start.2 = (bf16[1,32,7,7,512]{4,1,3,2,0:T(8,128)(2,1)S(1)}, bf16[1,32,7,7,512]{4,1,3,2,0:T(8,128)(2,1)}, u32[]{:S(2)}) copy-start(bf16[1,32,7,7,512]{4,1,3,2,0:T(8,128)(2,1)} %param.7) | copy-start | bytes 4816900
  25.1 5.3 %copy-start.1 = (bf16[1,32,7,7,512]{4,1,3,2,0:T(8,128)(2,1)S(1)}, bf16[1,32,7,7,512]{4,1,3,2,0:T(8,128)(2,1)}, u32[]{:S(2)}) copy-start(bf16[1,32,7,7,512]{4,1,3,2,0:T(8,128)(2,1)} %param.6) | copy-start | bytes 4816900
  25.1 5.3 %copy-start.3 = (bf16[1,32,7,7,512]{4,1,3,2,0:T(8,128)(2,1)S(1)}, bf16[1,32,7,7,512]{4,1,3,2,0:T(8,128)(2,1)}, u32[]{:S(2)}) copy-start(bf16[1,32,7,7,512]{4,1,3,2,0:T(8,128)(2,1)} %param.7) | copy-start | bytes 4816900
  36.2 12.0 %collective-permute-start.10 = (f32[8,32]{1,0:T(8,128)S(1)}, f32[8,32]{1,0:T(8,128)S(1)}, u32[]{:S(2)}, u32[]{:S(2)}) collective-permute-start(f32[8,32]{1,0:T(8,128)S(1)} %get-tuple-element.6), channel_id=1, source_target_pairs={{0,1},{1,0},{2,3},{3,2},{4,5},{5,4},{6,7},{7,6},{8,9},{9,8},{10,11... | collective-permute-start | bytes 3080 | tf_op jit(solution)/shard_map/ppermute | solution.py:133
  36.2 11.3 %all-to-all-start = ((f32[16,1,8]{2,1,0:T(1,128)}), f32[16,1,8]{2,1,0:T(1,128)S(1)}, u32[]{:S(2)}, u32[]{:S(2)}) async-start(f32[16,1,8]{2,1,0:T(1,128)} %bitcast.26), calls=%async_computation | async-start | bytes 16384 | tf_op jit(solution)/shard_map/all_to_all | solution.py:183

commit v2 on v0

v2 whole, which is shorter than its diff:
```python
import functools

import jax
import jax.numpy as jnp
from jax import lax
from jax.experimental import pallas as pl
from jax.experimental.pallas import tpu as pltpu
from jax.sharding import PartitionSpec as P

CHUNK = 4
HIGHEST = lax.Precision.HIGHEST


def nt_dot(a, b, precision=None):
    return lax.dot_general(
        a, b, (((1,), (1,)), ((), ())), precision=precision, preferred_element_type=jnp.float32
    )


def pack_test(act, grad):
    side, channels = act.shape[0], act.shape[2]
    maps = jnp.stack([act, grad])
    return jnp.pad(maps, ((0, 0), (0, 0), (0, 8 - side), (0, 0))).reshape(-1, channels)


def chunk_kernel(distances, first, last, side, scale, me_ref, *refs):
    number = len(distances)
    if not first:
        prev_ref, refs = refs[0], refs[1:]
    if last:
        weight_ref, ids, refs = refs[0], refs[1:3], refs[3:]
    tests, refs = refs[:number], refs[number:]
    train_act, train_grad, score_ref, refs = refs[:2], refs[2:4], refs[4], refs[5:]
    act_w, grad_w, raw, part, gram, sems = refs[-6:]
    if first:
        copies = [
            pltpu.make_async_copy(pair[1], kept, sems.at[k])
            for k, (pair, kept) in enumerate(zip((train_act, train_grad), refs))
        ]
        for copy in copies:
            copy.start()
        train_act, train_grad = (train_act[0], refs[0]), (train_grad[0], refs[1])
    head = (side - 1) * 8
    channels = act_w.shape[1]
    rows = train_act[0].shape[0] // (side * side)
    folds = 128 // (2 * rows)
    steps = 8 // folds

    seams = [tests[t][head : head + 16].astype(jnp.float32) for t in range(number)]
    for t in range(number):
        act_w[t * head : (t + 1) * head] = tests[t][:head]
        grad_w[t * head : (t + 1) * head] = tests[t][head + 16 :]
    act_seam = jnp.concatenate([seam[:8] for seam in seams], axis=0)
    grad_seam = jnp.concatenate([seam[8:] for seam in seams], axis=0)
    act_w[number * head :] = act_seam.astype(jnp.bfloat16)
    grad_w[number * head :] = grad_seam.astype(jnp.bfloat16)

    def at(t, u):
        start = t * head + u * 8 if u < side - 1 else number * head + t * 8
        return slice(start, start + 8)

    def grad_at(t, u):
        start = t * head + (u - 1) * 8 if u > 0 else number * head + t * 8
        return slice(start, start + 8)

    def trains(pair, block):
        a, b = divmod(block, side)
        pieces = []
        for fold in range(folds):
            place = ((a + fold * steps) * side + b) * rows
            if a + fold * steps < side:
                pieces += [half[place : place + rows] for half in pair]
            else:
                pieces.append(jnp.zeros((2 * rows, channels), jnp.bfloat16))
        return pieces

    def products(left, pair, out, block):
        both = jnp.concatenate(trains(pair, block) + trains(pair, block + 1), axis=0)
        got = nt_dot(left[...], both)
        out[block] = got[:, :128]
        out[block + 1] = got[:, 128:]

    def neighbour(a, b, shift, place):
        if 0 <= a + shift < steps:
            return raw[(a + shift) * side + b, place]
        wrapped = raw[((a + shift) % steps) * side + b, place]
        return pltpu.roll(wrapped, 128 - 2 * rows if shift > 0 else 2 * rows, 1)

    blocks = steps * side
    if first:
        copies[0].wait()
    for block in range(0, blocks, 2):
        products(act_w, train_act, raw, block)
    for a in range(steps):
        for b in range(side):
            for t in range(number):
                for u in range(side):
                    column = raw[a * side + b, at(t, u)]
                    if u < side - 1:
                        column += neighbour(a, b, 1, at(t, u + 1))
                    if u > 0:
                        column += neighbour(a, b, -1, at(t, u - 1))
                    part[a * side + b, at(t, u)] = column
    if first:
        copies[1].wait()
    totals = [jnp.zeros((8, 128), jnp.float32) for _ in range(number)]
    for block in range(0, blocks, 2):
        products(grad_w, train_grad, gram, block)
        for one in (block, block + 1):
            b = one % side
            for t in range(number):
                for u in range(side):
                    patch = part[one, at(t, u)]
                    if b < side - 1:
                        patch += pltpu.roll(part[one + 1, at(t, u)], 7, 0)
                    if b > 0:
                        patch += pltpu.roll(part[one - 1, at(t, u)], 1, 0)
                    totals[t] += patch * gram[one, grad_at(t, u)]

    tested = lax.broadcasted_iota(jnp.int32, score_ref.shape, 0) ^ me_ref[0]
    scores = jnp.zeros(score_ref.shape, jnp.float32) if first else prev_ref[...]
    for t in range(number):
        summed = jnp.sum(totals[t], axis=0, keepdims=True)
        score = summed
        for fold in range(1, folds):
            score += pltpu.roll(summed, 2 * rows * fold, 1)
        scores += jnp.where(tested == distances[t], score, 0.0)
    if not last:
        score_ref[...] = scores
        return
    influence = scores * (weight_ref[0] * scale)
    score_ref[...] = influence
    owned_ref = refs[0]
    owner = lax.broadcasted_iota(jnp.int32, (owned_ref.shape[0], rows), 0)
    owned = 0.0
    for half in range(2):
        hit = (owner == ids[half][...]).astype(jnp.float32)
        owned += nt_dot(hit, influence[:, half * rows : (half + 1) * rows], HIGHEST)
    owned_ref[...] = owned


def chunk_scores(distances, last, side, size, scale, me, weight, ids, prev, tests, acts, grads):
    first = prev is None
    rows, channels = acts[0].shape
    number = len(distances)
    height = number * side * 8
    folds = 128 // (2 * rows // (side * side))
    blocks = 8 // folds * side
    out_shape = [jax.ShapeDtypeStruct((size, 128), jnp.float32)]
    vmem, smem = pl.BlockSpec(memory_space=pltpu.VMEM), pl.BlockSpec(memory_space=pltpu.SMEM)
    args, in_specs = [me], [smem]
    if not first:
        args, in_specs = args + [prev], in_specs + [vmem]
    if last:
        args, in_specs = args + [weight, *ids], in_specs + [smem, vmem, vmem]
        out_shape.append(jax.ShapeDtypeStruct((size, size), jnp.float32))
    partner = vmem
    if first:
        out_shape += [jax.ShapeDtypeStruct((rows, channels), jnp.bfloat16)] * 2
        partner = pl.BlockSpec(memory_space=pl.ANY)
    args += [*tests, *acts, *grads]
    in_specs += [vmem] * number + [vmem, partner] * 2
    return pl.pallas_call(
        functools.partial(chunk_kernel, distances, first, last, side, scale),
        out_shape=out_shape,
        in_specs=in_specs,
        out_specs=[vmem] * len(out_shape),
        scratch_shapes=[
            pltpu.VMEM((height, channels), jnp.bfloat16),
            pltpu.VMEM((height, channels), jnp.bfloat16),
            pltpu.VMEM((blocks, height, 128), jnp.float32),
            pltpu.VMEM((blocks, height, 128), jnp.float32),
            pltpu.VMEM((blocks, height, 128), jnp.float32),
            pltpu.SemaphoreType.DMA((2,)),
        ],
        compiler_params=pltpu.CompilerParams(vmem_limit_bytes=16 * 1024 * 1024),
        cost_estimate=pl.CostEstimate(
            flops=4 * blocks * 128 * height * channels, bytes_accessed=0, transcendentals=0
        ),
        name="chunk_scores",
    )(*args)


def later_kernel(ids_ref, test_ref, out_ref):
    out_ref[...] = test_ref[...]


def after(test, ids):
    vmem = pl.BlockSpec(memory_space=pltpu.VMEM)
    return pl.pallas_call(
        later_kernel,
        out_shape=jax.ShapeDtypeStruct(test.shape, test.dtype),
        in_specs=[vmem, vmem],
        out_specs=vmem,
        compiler_params=pltpu.CompilerParams(vmem_limit_bytes=1024 * 1024),
        cost_estimate=pl.CostEstimate(flops=8_000_000_000, bytes_accessed=0, transcendentals=0),
        name="after",
    )(ids, test)


def across(x, distance):
    size = lax.axis_size("rows")
    return lax.ppermute(x, "rows", [(i, i ^ distance) for i in range(size)])


def gather_tests(own, later):
    size = lax.axis_size("rows")
    held = {0: own}
    if size == 16:
        held[8] = across(own, 8)
        held[4] = across(later, 4)
        held[2] = across(later, 2)
        held[14] = across(held[8], 6)
        held[12] = across(held[8], 4)
        held[10] = across(held[8], 2)
        held[6] = across(held[4], 2)
        return held, [[0, 8, 4, 2], [6, 10, 12, 14]]
    bit = 2
    while bit < size:
        for known in list(held):
            held[known ^ bit] = across(held[known], bit)
        bit *= 2
    known = sorted(held)
    return held, [known[i : i + CHUNK] for i in range(0, len(known), CHUNK)]


def body(train_act, train_grad, test_act, test_grad, ckpt_weights, owner_ids):
    tr_dev, side, channels = train_act.shape[1], train_act.shape[2], train_act.shape[4]
    size = lax.axis_size("rows")
    own_act = train_act[0].transpose(1, 2, 0, 3).reshape(-1, channels)
    own_grad = train_grad[0].transpose(1, 2, 0, 3).reshape(-1, channels)
    own_ids = owner_ids.reshape(1, tr_dev)
    ids = (own_ids, across(own_ids, 1))
    acts, grads = (own_act, across(own_act, 1)), (own_grad, across(own_grad, 1))

    own_test = pack_test(test_act[0, 0], test_grad[0, 0])
    later = after(own_test, ids[1])
    held, chunks = gather_tests(own_test, later)

    me = lax.axis_index("rows").reshape(1)
    scale = 1.0 / (3.0 * side * side * channels)
    done = [None]
    for k, distances in enumerate(chunks):
        last = k == len(chunks) - 1
        tests = [held[distance] for distance in distances]
        done = chunk_scores(
            distances, last, side, size, scale, me, ckpt_weights, ids, done[0], tests, acts, grads
        )
        if k == 0:
            acts, grads = (acts[0], done[1]), (grads[0], done[2])
    scores, packed = done

    received = lax.all_to_all(packed, "rows", split_axis=0, concat_axis=0, tiled=True)
    influence = scores[:, :tr_dev] + across(scores[:, tr_dev : 2 * tr_dev], 1)
    return influence.T, jnp.sum(received, axis=0, keepdims=True)


def solution(mesh):
    placed = (
        P(None, ("grp", "rows"), None, None, None),
        P(None, ("grp", "rows"), None, None, None),
        P(None, ("grp", "rows"), None, None, None),
        P(None, ("grp", "rows"), None, None, None),
        P(),
        P(("grp", "rows"), None),
    )
    return jax.shard_map(
        body,
        mesh=mesh,
        in_specs=placed,
        out_specs=(P(("grp", "rows"), None), P(("grp", "rows"), None)),
        check_vma=False,
    )
```

time: 110 us -> 40 us (0.36)
  blocking collectives: 55.8 us -> 0 us
  matrix products: 50.2 us -> 0 us
  starting transfers between devices: 0 us -> 19.2 us
  Pallas kernels: 0 us -> 9.19 us
  waiting for transfers between devices: 0 us -> 7.85 us
    dot_general x3 -> x0, matrix products: 50.2 us -> none  [the longest x1 40.5 us: pair_scores(): jnp.dot(tr_grad.reshape(-1, channels), te_grad.reshape(-1, channels).T, p...]
    all_gather x2 -> x0, blocking collectives: 46.4 us -> none  [the longest x1 26.1 us: body(): lax.all_gather(test_act, 'rows', axis=1, tiled=True)]
    ppermute x0 -> x11, starting transfers between devices: none -> 13.3 us  [across(): return lax.ppermute(x, 'rows', [(i, i ^ distance) for i in range(size)])]
    all_to_all x1 -> x0, blocking collectives: 9.44 us -> none  [body(): lax.all_to_all(packed, 'rows', split_axis=0, concat_axis=0, tiled=True)]
    pallas_call x0 -> x3, Pallas kernels: none -> 9.19 us  [the longest x2 8.55 us: chunk_scores(): pl.pallas_call(functools.partial(chunk_kernel, distances, first, last, si...]
    all_to_all x0 -> x1, waiting for transfers between devices: none -> 5.92 us  [body(): lax.all_to_all(packed, 'rows', split_axis=0, concat_axis=0, tiled=True)]
    all_to_all x0 -> x1, starting transfers between devices: none -> 5.88 us  [body(): lax.all_to_all(packed, 'rows', split_axis=0, concat_axis=0, tiled=True)]
    ppermute x0 -> x11, waiting for transfers between devices: none -> 1.93 us  [across(): return lax.ppermute(x, 'rows', [(i, i ^ distance) for i in range(size)])]
  transfers between devices with their start and end apart: 0 -> 12, of which waited for: 0 -> 2; matrix products, arithmetic and copies ran while one was open for 0% -> 4% of each run, Pallas kernels for 0% -> 14%
where the time goes in v2:
time: 40 us; the launch traced here: 39.8 us
  starting transfers between devices  19.2 us (48%)
  Pallas kernels  9.19 us (23%)
  waiting for transfers between devices  7.85 us (20%)
  other arithmetic  2.03 us (5%)
  between operations  1.4 us (4%)
    ppermute x11, starting transfers between devices, across(): return lax.ppermute(x, 'rows', [(i, i ^ distance) for i in range(size)])  13.3 us
    pallas_call x2, Pallas kernels, chunk_scores(): pl.pallas_call(functools.partial(chunk_kernel, distances, first, last, si...  8.55 us
    all_to_all x1, waiting for transfers between devices, body(): lax.all_to_all(packed, 'rows', split_axis=0, concat_axis=0, tiled=True)  5.92 us
    all_to_all x1, starting transfers between devices, body(): lax.all_to_all(packed, 'rows', split_axis=0, concat_axis=0, tiled=True)  5.88 us
    ppermute x11, waiting for transfers between devices, across(): return lax.ppermute(x, 'rows', [(i, i ^ distance) for i in range(size)])  1.93 us
    another operation x1, other arithmetic, pack_test(): maps = jnp.stack([act, grad])  0.88 us
  transfers between devices with their start and end apart: 12, of which 2 were waited for; matrix products, arithmetic and copies ran while one was open for 4% of the time, Pallas kernels for 14%

profile of v2, /device:TPU:0, one launch (start us, length us, event | category | flops | bytes accessed | tf_op | source)
XLA Modules:
  0.0 39.8 jit_solution(6601571529928682845)
XLA Ops:
  0.6 0.5 %collective-permute-start.4 = (bf16[1568,512]{1,0:T(8,128)(2,1)}, bf16[1568,512]{1,0:T(8,128)(2,1)}, u32[]{:S(2)}, u32[]{:S(2)}) collective-permute-start(bf16[1568,512]{1,0:T(8,128)(2,1)} %bitcast.21), channel_id=1, source_target_pairs={{0,1},{1,0},{2,3},{3,2},{4,5},{5,4},{6,7},{7,6},{8,9},{9,8},{10,11... | collective-permute-start | bytes 4816904 | tf_op jit(solution)/shard_map/ppermute | solution.py:203
  1.1 0.1 collective-permute-start.5
  1.2 0.4 %collective-permute-start.1 = (s32[1,32]{1,0:T(1,128)}, s32[1,32]{1,0:T(1,128)S(1)}, u32[]{:S(2)}, u32[]{:S(2)}) collective-permute-start(s32[1,32]{1,0:T(1,128)} %bitcast.30), channel_id=1, source_target_pairs={{0,1},{1,0},{2,3},{3,2},{4,5},{5,4},{6,7},{7,6},{8,9},{9,8},{10,11... | collective-permute-start | bytes 392 | tf_op jit(solution)/shard_map/ppermute | solution.py:203
  1.7 0.9 %fusion.2 = bf16[2,7,8,512]{3,2,1,0:T(8,128)(2,1)S(1)} fusion(bf16[1,7,7,512]{3,2,1,0:T(8,128)(2,1)} %bitcast.32, bf16[1,7,7,512]{3,2,1,0:T(8,128)(2,1)} %bitcast.33), kind=kLoop, calls=%fused_computation.3 | loop fusion | flops 401408 | bytes 215040 | tf_op jit(solution)/shard_map/stack | solution.py:22
  2.5 0.0 copy-start
  2.6 0.0 copy-start.1
  2.6 3.7 %collective-permute-start = (bf16[112,512]{1,0:T(8,128)(2,1)S(1)}, bf16[112,512]{1,0:T(8,128)(2,1)S(1)}, u32[]{:S(2)}, u32[]{:S(2)}) collective-permute-start(bf16[112,512]{1,0:T(8,128)(2,1)S(1)} %bitcast.27), channel_id=1, source_target_pairs={{0,8},{1,9},{2,10},{3,11},{4,12},{5,13},{6,14},{7,15},{8,0},{9,1},... | collective-permute-start | bytes 344072 | tf_op jit(solution)/shard_map/ppermute | solution.py:203
  6.3 0.6 %after.1 = bf16[112,512]{1,0:T(8,128)(2,1)} custom-call(s32[1,32]{1,0:T(1,128)S(1)} %collective-permute-done.1.ids_ref.refs_3_, bf16[112,512]{1,0:T(8,128)(2,1)S(1)} %bitcast.28), custom_call_target="tpu_custom_call" | custom-call | flops 8000000000 | tf_op jit(solution)/shard_map/after/pallas_call | solution.py:190
  7.0 1.6 %collective-permute-start.2 = (bf16[112,512]{1,0:T(8,128)(2,1)}, bf16[112,512]{1,0:T(8,128)(2,1)S(1)}, u32[]{:S(2)}, u32[]{:S(2)}) collective-permute-start(bf16[112,512]{1,0:T(8,128)(2,1)} %after.1), channel_id=1, source_target_pairs={{0,4},{1,5},{2,6},{3,7},{4,0},{5,1},{6,2},{7,3},{8,12},{9,13},{10,... | collective-permute-start | bytes 344072 | tf_op jit(solution)/shard_map/ppermute | solution.py:203
  8.5 1.5 %collective-permute-start.3 = (bf16[112,512]{1,0:T(8,128)(2,1)}, bf16[112,512]{1,0:T(8,128)(2,1)}, u32[]{:S(2)}, u32[]{:S(2)}) collective-permute-start(bf16[112,512]{1,0:T(8,128)(2,1)} %after.1), channel_id=1, source_target_pairs={{0,2},{1,3},{2,0},{3,1},{4,6},{5,7},{6,4},{7,5},{8,10},{9,11},{10,... | collective-permute-start | bytes 344072 | tf_op jit(solution)/shard_map/ppermute | solution.py:203
  10.7 1.9 %collective-permute-done.refs_1_ = bf16[112,512]{1,0:T(8,128)(2,1)S(1)} collective-permute-done((bf16[112,512]{1,0:T(8,128)(2,1)S(1)}, bf16[112,512]{1,0:T(8,128)(2,1)S(1)}, u32[]{:S(2)}, u32[]{:S(2)}) %collective-permute-start) | collective-permute-done | bytes 114720 | tf_op jit(solution)/shard_map/ppermute | solution.py:203
  12.6 1.6 %collective-permute-start.7 = (bf16[112,512]{1,0:T(8,128)(2,1)S(1)}, bf16[112,512]{1,0:T(8,128)(2,1)S(1)}, u32[]{:S(2)}, u32[]{:S(2)}) collective-permute-start(bf16[112,512]{1,0:T(8,128)(2,1)S(1)} %collective-permute-done.refs_1_), channel_id=1, source_target_pairs={{0,2},{1,3},{2,0},{3,1},{4,6},{5,7},{6,4},{7,5},{8,10},{9,11},{10,... | collective-permute-start | bytes 344072 | tf_op jit(solution)/shard_map/ppermute | solution.py:203
  14.2 0.6 %collective-permute-start.8 = (bf16[112,512]{1,0:T(8,128)(2,1)S(1)}, bf16[112,512]{1,0:T(8,128)(2,1)S(1)}, u32[]{:S(2)}, u32[]{:S(2)}) collective-permute-start(bf16[112,512]{1,0:T(8,128)(2,1)S(1)} %collective-permute-done.refs_1_), channel_id=1, source_target_pairs={{0,4},{1,5},{2,6},{3,7},{4,0},{5,1},{6,2},{7,3},{8,12},{9,13},{10,... | collective-permute-start | bytes 344072 | tf_op jit(solution)/shard_map/ppermute | solution.py:203
  14.8 1.9 %collective-permute-start.9 = (bf16[112,512]{1,0:T(8,128)(2,1)S(1)}, bf16[112,512]{1,0:T(8,128)(2,1)S(1)}, u32[]{:S(2)}, u32[]{:S(2)}) collective-permute-start(bf16[112,512]{1,0:T(8,128)(2,1)S(1)} %collective-permute-done.refs_1_), channel_id=1, source_target_pairs={{0,6},{1,7},{2,4},{3,5},{4,2},{5,3},{6,0},{7,1},{8,14},{9,15},{10,... | collective-permute-start | bytes 344072 | tf_op jit(solution)/shard_map/ppermute | solution.py:203
  16.7 1.0 %collective-permute-start.6 = (bf16[112,512]{1,0:T(8,128)(2,1)S(1)}, bf16[112,512]{1,0:T(8,128)(2,1)S(1)}, u32[]{:S(2)}, u32[]{:S(2)}) collective-permute-start(bf16[112,512]{1,0:T(8,128)(2,1)S(1)} %collective-permute-done.2.refs_2_), channel_id=1, source_target_pairs={{0,2},{1,3},{2,0},{3,1},{4,6},{5,7},{6,4},{7,5},{8,10},{9,11},{10,... | collective-permute-start | bytes 344072 | tf_op jit(solution)/shard_map/ppermute | solution.py:203
  17.7 0.0 copy-start.2
  17.7 5.1 %chunk_scores.2 = (f32[16,128]{1,0:T(8,128)S(1)}, bf16[1568,512]{1,0:T(8,128)(2,1)S(1)}, bf16[1568,512]{1,0:T(8,128)(2,1)S(1)}) custom-call(s32[1]{0:T(128)} %bitcast.me_ref, bf16[112,512]{1,0:T(8,128)(2,1)S(1)} %bitcast.29, bf16[112,512]{1,0:T(8,128)(2,1)S(1)} %collective-permute-done.refs_1_, bf16[112,512]{1,0:T(8,128)(2,1)S(1)} %collective-permute-done.2.refs_2_, ...), custom_call_target="tpu_custom_call" | custom-call | flops 1644167168 | tf_op jit(solution)/shard_map/chunk_scores/pallas_call | solution.py:163
  22.9 3.5 %chunk_scores.3 = (f32[16,128]{1,0:T(8,128)S(1)}, f32[16,16]{1,0:T(8,128)}) custom-call(s32[1]{0:T(128)} %bitcast.me_ref, f32[16,128]{1,0:T(8,128)S(1)} %get-tuple-element.7.refs_0_, f32[1]{0:T(128)S(6)} %copy.9.refs_1_, s32[1,32]{1,0:T(1,128)S(1)} %bitcast.31, s32[1,32]{1,0:T(1,128)S(1)} %copy-done.4, bf16[112,512]{1,0:T(8,128)(2,1)S(1)} %collective-permute-done.6.refs_4_, ...), custom_call_target="tpu_custom_call" | custom-call | flops 1644167168 | tf_op jit(solution)/shard_map/chunk_scores/pallas_call | solution.py:163
  26.4 0.1 slice.7
  26.4 5.9 %all-to-all-start = ((f32[16,1,16]{2,1,0:T(1,128)}), f32[16,1,16]{2,1,0:T(1,128)S(1)}, u32[]{:S(2)}, u32[]{:S(2)}) async-start(f32[16,1,16]{2,1,0:T(1,128)} %bitcast.17), calls=%async_computation | async-start | bytes 16384 | tf_op jit(solution)/shard_map/all_to_all | solution.py:253
  32.3 0.4 %collective-permute-start.10 = (f32[16,32]{1,0:T(8,128)S(1)}, f32[16,32]{1,0:T(8,128)S(1)}, u32[]{:S(2)}, u32[]{:S(2)}) collective-permute-start(f32[16,32]{1,0:T(8,128)S(1)} %slice.7), channel_id=1, source_target_pairs={{0,1},{1,0},{2,3},{3,2},{4,5},{5,4},{6,7},{7,6},{8,9},{9,8},{10,11... | collective-permute-start | bytes 6152 | tf_op jit(solution)/shard_map/ppermute | solution.py:203
  32.7 5.9 %all-to-all-done = f32[16,1,16]{2,1,0:T(1,128)S(1)} async-done(((f32[16,1,16]{2,1,0:T(1,128)}), f32[16,1,16]{2,1,0:T(1,128)S(1)}, u32[]{:S(2)}, u32[]{:S(2)}) %all-to-all-start) | async-done | bytes 1056 | tf_op jit(solution)/shard_map/all_to_all | solution.py:253
  38.6 0.5 %reduce_sum.9 = f32[16]{0:T(128)} reduce(f32[16,1,16]{2,1,0:T(1,128)S(1)} %all-to-all-done, f32[]{:T(128)} %constant.8.clone.1), dimensions={0,1}, to_apply=%region_0.1 | reduce | flops 240 | bytes 1092 | tf_op jit(solution)/shard_map/reduce_sum | solution.py:255
  39.2 0.6 %add_bitcast_fusion = f32[32,16]{0,1:T(8,128)} fusion(f32[16,32]{1,0:T(8,128)S(1)} %collective-permute-done.10, f32[16,128]{1,0:T(8,128)S(1)} %get-tuple-element.10), kind=kLoop, calls=%fused_computation.4 | loop fusion | flops 512 | bytes 6144 | tf_op jit(solution)/shard_map/transpose | solution.py:255
  (17 shorter events, 0.0 us)
Async XLA Ops:
  0.6 16.1 %collective-permute-start.4 = (bf16[1568,512]{1,0:T(8,128)(2,1)}, bf16[1568,512]{1,0:T(8,128)(2,1)}, u32[]{:S(2)}, u32[]{:S(2)}) collective-permute-start(bf16[1568,512]{1,0:T(8,128)(2,1)} %bitcast.21), channel_id=1, source_target_pairs={{0,1},{1,0},{2,3},{3,2},{4,5},{5,4},{6,7},{7,6},{8,9},{9,8},{10,11... | collective-permute-start | bytes 4816904 | tf_op jit(solution)/shard_map/ppermute | solution.py:203
  1.1 16.5 %collective-permute-start.5 = (bf16[1568,512]{1,0:T(8,128)(2,1)}, bf16[1568,512]{1,0:T(8,128)(2,1)}, u32[]{:S(2)}, u32[]{:S(2)}) collective-permute-start(bf16[1568,512]{1,0:T(8,128)(2,1)} %bitcast.24), channel_id=1, source_target_pairs={{0,1},{1,0},{2,3},{3,2},{4,5},{5,4},{6,7},{7,6},{8,9},{9,8},{10,11... | collective-permute-start | bytes 4816904 | tf_op jit(solution)/shard_map/ppermute | solution.py:203
  1.2 5.1 %collective-permute-start.1 = (s32[1,32]{1,0:T(1,128)}, s32[1,32]{1,0:T(1,128)S(1)}, u32[]{:S(2)}, u32[]{:S(2)}) collective-permute-start(s32[1,32]{1,0:T(1,128)} %bitcast.30), channel_id=1, source_target_pairs={{0,1},{1,0},{2,3},{3,2},{4,5},{5,4},{6,7},{7,6},{8,9},{9,8},{10,11... | collective-permute-start | bytes 392 | tf_op jit(solution)/shard_map/ppermute | solution.py:203
  2.5 15.1 %copy-start = (bf16[1,32,7,7,512]{4,1,3,2,0:T(8,128)(2,1)S(1)}, bf16[1,32,7,7,512]{4,1,3,2,0:T(8,128)(2,1)}, u32[]{:S(2)}) copy-start(bf16[1,32,7,7,512]{4,1,3,2,0:T(8,128)(2,1)} %param.6) | copy-start | bytes 4816900
  2.6 15.1 %copy-start.1 = (bf16[1,32,7,7,512]{4,1,3,2,0:T(8,128)(2,1)S(1)}, bf16[1,32,7,7,512]{4,1,3,2,0:T(8,128)(2,1)}, u32[]{:S(2)}) copy-start(bf16[1,32,7,7,512]{4,1,3,2,0:T(8,128)(2,1)} %param.7) | copy-start | bytes 4816900
  2.6 10.0 %collective-permute-start = (bf16[112,512]{1,0:T(8,128)(2,1)S(1)}, bf16[112,512]{1,0:T(8,128)(2,1)S(1)}, u32[]{:S(2)}, u32[]{:S(2)}) collective-permute-start(bf16[112,512]{1,0:T(8,128)(2,1)S(1)} %bitcast.27), channel_id=1, source_target_pairs={{0,8},{1,9},{2,10},{3,11},{4,12},{5,13},{6,14},{7,15},{8,0},{9,1},... | collective-permute-start | bytes 344072 | tf_op jit(solution)/shard_map/ppermute | solution.py:203
  6.3 0.6 %copy-start.3 = (s32[1,32]{1,0:T(1,128)}, s32[1,32]{1,0:T(1,128)S(1)}, u32[]{:S(2)}) copy-start(s32[1,32]{1,0:T(1,128)S(1)} %collective-permute-done.1.ids_ref.refs_3_) | copy-start | bytes 388
  7.0 7.2 %collective-permute-start.2 = (bf16[112,512]{1,0:T(8,128)(2,1)}, bf16[112,512]{1,0:T(8,128)(2,1)S(1)}, u32[]{:S(2)}, u32[]{:S(2)}) collective-permute-start(bf16[112,512]{1,0:T(8,128)(2,1)} %after.1), channel_id=1, source_target_pairs={{0,4},{1,5},{2,6},{3,7},{4,0},{5,1},{6,2},{7,3},{8,12},{9,13},{10,... | collective-permute-start | bytes 344072 | tf_op jit(solution)/shard_map/ppermute | solution.py:203
  8.5 6.3 %collective-permute-start.3 = (bf16[112,512]{1,0:T(8,128)(2,1)}, bf16[112,512]{1,0:T(8,128)(2,1)}, u32[]{:S(2)}, u32[]{:S(2)}) collective-permute-start(bf16[112,512]{1,0:T(8,128)(2,1)} %after.1), channel_id=1, source_target_pairs={{0,2},{1,3},{2,0},{3,1},{4,6},{5,7},{6,4},{7,5},{8,10},{9,11},{10,... | collective-permute-start | bytes 344072 | tf_op jit(solution)/shard_map/ppermute | solution.py:203
  12.6 10.2 %collective-permute-start.7 = (bf16[112,512]{1,0:T(8,128)(2,1)S(1)}, bf16[112,512]{1,0:T(8,128)(2,1)S(1)}, u32[]{:S(2)}, u32[]{:S(2)}) collective-permute-start(bf16[112,512]{1,0:T(8,128)(2,1)S(1)} %collective-permute-done.refs_1_), channel_id=1, source_target_pairs={{0,2},{1,3},{2,0},{3,1},{4,6},{5,7},{6,4},{7,5},{8,10},{9,11},{10,... | collective-permute-start | bytes 344072 | tf_op jit(solution)/shard_map/ppermute | solution.py:203
  14.2 8.7 %collective-permute-start.8 = (bf16[112,512]{1,0:T(8,128)(2,1)S(1)}, bf16[112,512]{1,0:T(8,128)(2,1)S(1)}, u32[]{:S(2)}, u32[]{:S(2)}) collective-permute-start(bf16[112,512]{1,0:T(8,128)(2,1)S(1)} %collective-permute-done.refs_1_), channel_id=1, source_target_pairs={{0,4},{1,5},{2,6},{3,7},{4,0},{5,1},{6,2},{7,3},{8,12},{9,13},{10,... | collective-permute-start | bytes 344072 | tf_op jit(solution)/shard_map/ppermute | solution.py:203
  14.8 8.0 %collective-permute-start.9 = (bf16[112,512]{1,0:T(8,128)(2,1)S(1)}, bf16[112,512]{1,0:T(8,128)(2,1)S(1)}, u32[]{:S(2)}, u32[]{:S(2)}) collective-permute-start(bf16[112,512]{1,0:T(8,128)(2,1)S(1)} %collective-permute-done.refs_1_), channel_id=1, source_target_pairs={{0,6},{1,7},{2,4},{3,5},{4,2},{5,3},{6,0},{7,1},{8,14},{9,15},{10,... | collective-permute-start | bytes 344072 | tf_op jit(solution)/shard_map/ppermute | solution.py:203
  16.7 6.2 %collective-permute-start.6 = (bf16[112,512]{1,0:T(8,128)(2,1)S(1)}, bf16[112,512]{1,0:T(8,128)(2,1)S(1)}, u32[]{:S(2)}, u32[]{:S(2)}) collective-permute-start(bf16[112,512]{1,0:T(8,128)(2,1)S(1)} %collective-permute-done.2.refs_2_), channel_id=1, source_target_pairs={{0,2},{1,3},{2,0},{3,1},{4,6},{5,7},{6,4},{7,5},{8,10},{9,11},{10,... | collective-permute-start | bytes 344072 | tf_op jit(solution)/shard_map/ppermute | solution.py:203
  17.7 5.2 %copy-start.2 = (s32[32,1]{0,1:T(1,128)S(1)}, s32[32,1]{0,1:T(1,128)}, u32[]{:S(2)}) copy-start(s32[32,1]{0,1:T(1,128)} %param.11) | copy-start | bytes 388
  17.7 5.2 %copy-start.4 = (s32[1,32]{1,0:T(1,128)S(1)}, s32[1,32]{1,0:T(1,128)}, u32[]{:S(2)}) copy-start(s32[1,32]{1,0:T(1,128)} %copy-done.3) | copy-start | bytes 388
  26.4 12.2 %all-to-all-start = ((f32[16,1,16]{2,1,0:T(1,128)}), f32[16,1,16]{2,1,0:T(1,128)S(1)}, u32[]{:S(2)}, u32[]{:S(2)}) async-start(f32[16,1,16]{2,1,0:T(1,128)} %bitcast.17), calls=%async_computation | async-start | bytes 16384 | tf_op jit(solution)/shard_map/all_to_all | solution.py:253
  32.3 6.9 %collective-permute-start.10 = (f32[16,32]{1,0:T(8,128)S(1)}, f32[16,32]{1,0:T(8,128)S(1)}, u32[]{:S(2)}, u32[]{:S(2)}) collective-permute-start(f32[16,32]{1,0:T(8,128)S(1)} %slice.7), channel_id=1, source_target_pairs={{0,1},{1,0},{2,3},{3,2},{4,5},{5,4},{6,7},{7,6},{8,9},{9,8},{10,11... | collective-permute-start | bytes 6152 | tf_op jit(solution)/shard_map/ppermute | solution.py:203

commit v3 on v2

v3 whole, which is shorter than its diff:
```python
import functools

import jax
import jax.numpy as jnp
from jax import lax
from jax.experimental import pallas as pl
from jax.experimental.pallas import tpu as pltpu
from jax.sharding import PartitionSpec as P

CHUNK = 4
HIGHEST = lax.Precision.HIGHEST


def nt_dot(a, b, precision=None):
    return lax.dot_general(
        a, b, (((1,), (1,)), ((), ())), precision=precision, preferred_element_type=jnp.float32
    )


def pack_test(act, grad):
    side, channels = act.shape[0], act.shape[2]
    maps = jnp.stack([act, grad])
    return jnp.pad(maps, ((0, 0), (0, 0), (0, 8 - side), (0, 0))).reshape(-1, channels)


def chunk_kernel(distances, places, first, last, side, scale, me_ref, *refs):
    number = len(distances)
    if not first:
        prev_ref, refs = refs[0], refs[1:]
    if last:
        weight_ref, ids, refs = refs[0], refs[1], refs[2:]
    arrays = 1 + max(array for array, _ in places)
    tests, refs = refs[:arrays], refs[arrays:]
    train_act, train_grad, score_ref, refs = refs[0], refs[1], refs[2], refs[3:]
    act_w, grad_w, raw, part, gram = refs[-5:]
    head = (side - 1) * 8
    channels = act_w.shape[1]
    rows = train_act.shape[0] // (side * side)
    folds = 128 // rows
    steps = 8 // folds

    def test_rows(t, start, stop):
        array, place = places[t]
        return tests[array][place + start : place + stop]

    seams = [test_rows(t, head, head + 16).astype(jnp.float32) for t in range(number)]
    for t in range(number):
        act_w[t * head : (t + 1) * head] = test_rows(t, 0, head)
        grad_w[t * head : (t + 1) * head] = test_rows(t, head + 16, 2 * head + 16)
    act_seam = jnp.concatenate([seam[:8] for seam in seams], axis=0)
    grad_seam = jnp.concatenate([seam[8:] for seam in seams], axis=0)
    act_w[number * head :] = act_seam.astype(jnp.bfloat16)
    grad_w[number * head :] = grad_seam.astype(jnp.bfloat16)

    def at(t, u):
        start = t * head + u * 8 if u < side - 1 else number * head + t * 8
        return slice(start, start + 8)

    def grad_at(t, u):
        start = t * head + (u - 1) * 8 if u > 0 else number * head + t * 8
        return slice(start, start + 8)

    def trains(source, block):
        a, b = divmod(block, side)
        pieces = []
        for fold in range(folds):
            place = ((a + fold * steps) * side + b) * rows
            if a + fold * steps < side:
                pieces.append(source[place : place + rows])
            else:
                pieces.append(jnp.zeros((rows, channels), jnp.bfloat16))
        return pieces

    def products(left, pair, out, block):
        both = jnp.concatenate(trains(pair, block) + trains(pair, block + 1), axis=0)
        got = nt_dot(left[...], both)
        out[block] = got[:, :128]
        out[block + 1] = got[:, 128:]

    def neighbour(a, b, shift, place):
        if 0 <= a + shift < steps:
            return raw[(a + shift) * side + b, place]
        wrapped = raw[((a + shift) % steps) * side + b, place]
        return pltpu.roll(wrapped, 128 - rows if shift > 0 else rows, 1)

    blocks = steps * side
    totals = [jnp.zeros((8, 128), jnp.float32) for _ in range(number)]

    def dy_sum(a):
        for b in range(side):
            for t in range(number):
                for u in range(side):
                    column = raw[a * side + b, at(t, u)]
                    if u < side - 1:
                        column += neighbour(a, b, 1, at(t, u + 1))
                    if u > 0:
                        column += neighbour(a, b, -1, at(t, u - 1))
                    part[a * side + b, at(t, u)] = column

    def score(one):
        b = one % side
        for t in range(number):
            for u in range(side):
                patch = part[one, at(t, u)]
                if b < side - 1:
                    patch += pltpu.roll(part[one + 1, at(t, u)], 7, 0)
                if b > 0:
                    patch += pltpu.roll(part[one - 1, at(t, u)], 1, 0)
                totals[t] += patch * gram[one, grad_at(t, u)]

    raw_order = list(range(0, blocks, 2))
    grams = list(range(0, blocks, 2))
    made, summed, scored, gram_made = set(), 0, 0, 0
    for block in raw_order:
        products(act_w, train_act, raw, block)
        made |= {block, block + 1}
        while summed < steps and all(
            a % steps * side + b in made for a in (summed - 1, summed, summed + 1) for b in range(side)
        ):
            dy_sum(summed)
            summed += 1
    for block in grams:
        products(grad_w, train_grad, gram, block)
        while scored < block + 2 and (scored // side + 1) <= summed:
            score(scored)
            scored += 1
    assert summed == steps and scored == blocks

    tested = lax.broadcasted_iota(jnp.int32, score_ref.shape, 0) ^ me_ref[0]
    scores = jnp.zeros(score_ref.shape, jnp.float32) if first else prev_ref[...]
    for t in range(number):
        summed = jnp.sum(totals[t], axis=0, keepdims=True)
        score = summed
        for fold in range(1, folds):
            score += pltpu.roll(summed, rows * fold, 1)
        scores += jnp.where(tested == distances[t], score, 0.0)
    if not last:
        score_ref[...] = scores
        return
    influence = scores * (weight_ref[0] * scale)
    score_ref[...] = influence
    owned_ref = refs[0]
    owner = lax.broadcasted_iota(jnp.int32, (owned_ref.shape[0], rows), 0)
    hit = (owner == ids[...]).astype(jnp.float32)
    owned_ref[...] = nt_dot(hit, influence[:, :rows], HIGHEST)


def chunk_scores(distances, places, last, side, size, scale, me, weight, ids, prev, tests, act, grad):
    first = prev is None
    rows, channels = act.shape
    height = len(distances) * side * 8
    blocks = 8 // (128 // (rows // (side * side))) * side
    out_shape = [jax.ShapeDtypeStruct((size, 128), jnp.float32)]
    vmem, smem = pl.BlockSpec(memory_space=pltpu.VMEM), pl.BlockSpec(memory_space=pltpu.SMEM)
    args, in_specs = [me], [smem]
    if not first:
        args, in_specs = args + [prev], in_specs + [vmem]
    if last:
        args, in_specs = args + [weight, ids], in_specs + [smem, vmem]
        out_shape.append(jax.ShapeDtypeStruct((size, size), jnp.float32))
    args, in_specs = args + [*tests, act, grad], in_specs + [vmem] * (len(tests) + 2)
    return pl.pallas_call(
        functools.partial(chunk_kernel, distances, places, first, last, side, scale),
        out_shape=out_shape,
        in_specs=in_specs,
        out_specs=[vmem] * len(out_shape),
        scratch_shapes=[
            pltpu.VMEM((height, channels), jnp.bfloat16),
            pltpu.VMEM((height, channels), jnp.bfloat16),
            pltpu.VMEM((blocks, height, 128), jnp.float32),
            pltpu.VMEM((blocks, height, 128), jnp.float32),
            pltpu.VMEM((blocks, height, 128), jnp.float32),
        ],
        compiler_params=pltpu.CompilerParams(vmem_limit_bytes=24 * 1024 * 1024),
        cost_estimate=pl.CostEstimate(
            flops=4 * blocks * 128 * height * channels, bytes_accessed=0, transcendentals=0
        ),
        name="chunk_scores",
    )(*args)


def across(x, distance):
    size = lax.axis_size("rows")
    return lax.ppermute(x, "rows", [(i, i ^ distance) for i in range(size)])


def gather_tests(own):
    size, height = lax.axis_size("rows"), own.shape[0]
    held = {0: own}
    other = across(own, 1)
    if size == 16:
        later, other = lax.optimization_barrier((own, other))
        held[8] = across(own, 8)
        held[4] = across(later, 4)
        held[2] = across(later, 2)
        held[6] = across(later, 6)
        held[14] = across(held[8], 6)
        held[12] = across(held[8], 4)
        held[10] = across(held[8], 2)
        groups = [[0, 2, 4, 6], [8, 10, 12, 14]]
    else:
        bit = 2
        while bit < size:
            for known in list(held):
                held[known ^ bit] = across(held[known], bit)
            bit *= 2
        groups = [list(range(i, i + 2 * CHUNK, 2)) for i in range(0, size, 2 * CHUNK)]
    return held, other, groups


def body(train_act, train_grad, test_act, test_grad, ckpt_weights, owner_ids):
    tr_dev, side, channels = train_act.shape[1], train_act.shape[2], train_act.shape[4]
    size = lax.axis_size("rows")
    act = train_act[0].transpose(1, 2, 0, 3).reshape(-1, channels)
    grad = train_grad[0].transpose(1, 2, 0, 3).reshape(-1, channels)
    ids = owner_ids.reshape(1, tr_dev)
    held, other, groups = gather_tests(pack_test(test_act[0, 0], test_grad[0, 0]))

    me = lax.axis_index("rows").reshape(1)
    scale = 1.0 / (3.0 * side * side * channels)
    scores, came, sent_on = None, {1: other}, {}
    for k in range(len(groups) + 1):
        last, group = k == len(groups), groups[k] if k < len(groups) else []
        if k != 1 or len(groups) > 2:
            came, sent_on = came | sent_on, {}
        distances, arrays = group + list(came), [held[d] for d in group] + list(came.values())
        late = group[1:] if k else []
        if late:
            *sent, scores = lax.optimization_barrier((*[held[d] for d in late], scores))
        sent = dict(zip(late, sent)) if late else {}
        came = {}
        sent_on |= {d ^ 1: across(sent.get(d, held[d]), 1) for d in group if d}
        places = [(test, 0) for test in range(len(arrays))]
        done = chunk_scores(
            distances, places, last, side, size, scale, me, ckpt_weights, ids, scores, arrays, act, grad
        )
        scores = done[0]
    scores, packed = done
    received = lax.all_to_all(packed, "rows", split_axis=0, concat_axis=0, tiled=True)
    return scores[:, :tr_dev].T, jnp.sum(received, axis=0, keepdims=True)


def solution(mesh):
    placed = (
        P(None, ("grp", "rows"), None, None, None),
        P(None, ("grp", "rows"), None, None, None),
        P(None, ("grp", "rows"), None, None, None),
        P(None, ("grp", "rows"), None, None, None),
        P(),
        P(("grp", "rows"), None),
    )
    return jax.shard_map(
        body,
        mesh=mesh,
        in_specs=placed,
        out_specs=(P(("grp", "rows"), None), P(("grp", "rows"), None)),
        check_vma=False,
    )
```

time: 40 us -> 39.4 us (0.985)
  Pallas kernels: 9.19 us -> 5.47 us
  local copies, waits for them, and re-layouts: 0.1 us -> 3.45 us
  waiting for transfers between devices: 7.85 us -> 9.12 us
  starting transfers between devices: 19.2 us -> 18.3 us
  other arithmetic: 2.03 us -> 1.43 us
    pallas_call x3, Pallas kernels: 9.19 us -> 5.47 us  [chunk_scores(): pl.pallas_call(functools.partial(chunk_kernel, distances, places, first,...]
    unnamed x10, local copies, waits for them, and re-layouts: 0.03 us -> 2.85 us
    ppermute x11 -> x15, waiting for transfers between devices: 1.93 us -> 3.33 us  [across(): return lax.ppermute(x, 'rows', [(i, i ^ distance) for i in range(size)])]
    transpose x1 -> x0, other arithmetic: 0.6 us -> none  [body(): return (influence.T, jnp.sum(received, axis=0, keepdims=True))]
    transpose x0 -> x1, local copies, waits for them, and re-layouts: none -> 0.6 us  [body(): return (scores[:, :tr_dev].T, jnp.sum(received, axis=0, keepdims=True))]
    ppermute x11 -> x15, starting transfers between devices: 13.3 us -> 12.8 us  [across(): return lax.ppermute(x, 'rows', [(i, i ^ distance) for i in range(size)])]
    all_to_all x1, starting transfers between devices: 5.88 us -> 5.44 us  [body(): lax.all_to_all(packed, 'rows', split_axis=0, concat_axis=0, tiled=True)]
  transfers between devices with their start and end apart: 12 -> 16, of which waited for: 2 -> 3; matrix products, arithmetic and copies ran while one was open for 4% -> 2% of each run, Pallas kernels for 14% -> 7%
where the time goes in v3:
time: 39.4 us; the launch traced here: 39.2 us
  starting transfers between devices  18.3 us (46%)
  waiting for transfers between devices  9.12 us (23%)
  Pallas kernels  5.47 us (14%)
  local copies, waits for them, and re-layouts  3.45 us (9%)
  other arithmetic  1.43 us (4%)
  between operations  1.42 us (4%)
    ppermute x15, starting transfers between devices, across(): return lax.ppermute(x, 'rows', [(i, i ^ distance) for i in range(size)])  12.8 us
    all_to_all x1, waiting for transfers between devices, body(): lax.all_to_all(packed, 'rows', split_axis=0, concat_axis=0, tiled=True)  5.8 us
    pallas_call x3, Pallas kernels, chunk_scores(): pl.pallas_call(functools.partial(chunk_kernel, distances, places, first,...  5.47 us
    all_to_all x1, starting transfers between devices, body(): lax.all_to_all(packed, 'rows', split_axis=0, concat_axis=0, tiled=True)  5.44 us
    ppermute x15, waiting for transfers between devices, across(): return lax.ppermute(x, 'rows', [(i, i ^ distance) for i in range(size)])  3.33 us
    unnamed x10, local copies, waits for them, and re-layouts  2.85 us
    another operation x1, other arithmetic, pack_test(): maps = jnp.stack([act, grad])  0.89 us
  transfers between devices with their start and end apart: 16, of which 3 were waited for; matrix products, arithmetic and copies ran while one was open for 2% of the time, Pallas kernels for 7%

profile of v3, /device:TPU:0, one launch (start us, length us, event | category | flops | bytes accessed | tf_op | source)
XLA Modules:
  0.0 39.2 jit_solution(10637721515563751246)
XLA Ops:
  0.6 0.9 %fusion.2 = bf16[2,7,8,512]{3,2,1,0:T(8,128)(2,1)S(1)} fusion(bf16[1,7,7,512]{3,2,1,0:T(8,128)(2,1)} %bitcast.34, bf16[1,7,7,512]{3,2,1,0:T(8,128)(2,1)} %bitcast.35), kind=kLoop, calls=%fused_computation.3 | loop fusion | flops 401408 | bytes 215040 | tf_op jit(solution)/shard_map/stack | solution.py:22
  1.5 0.5 %collective-permute-start.4 = (bf16[112,512]{1,0:T(8,128)(2,1)S(1)}, bf16[112,512]{1,0:T(8,128)(2,1)S(1)}, u32[]{:S(2)}, u32[]{:S(2)}) collective-permute-start(bf16[112,512]{1,0:T(8,128)(2,1)S(1)} %bitcast.27), channel_id=1, source_target_pairs={{0,1},{1,0},{2,3},{3,2},{4,5},{5,4},{6,7},{7,6},{8,9},{9,8},{10,11... | collective-permute-start | bytes 344072 | tf_op jit(solution)/shard_map/ppermute | solution.py:184
  2.0 3.7 %collective-permute-start = (bf16[112,512]{1,0:T(8,128)(2,1)S(1)}, bf16[112,512]{1,0:T(8,128)(2,1)S(1)}, u32[]{:S(2)}, u32[]{:S(2)}) collective-permute-start(bf16[112,512]{1,0:T(8,128)(2,1)S(1)} %bitcast.28), channel_id=1, source_target_pairs={{0,8},{1,9},{2,10},{3,11},{4,12},{5,13},{6,14},{7,15},{8,0},{9,1},... | collective-permute-start | bytes 344072 | tf_op jit(solution)/shard_map/ppermute | solution.py:184
  5.7 2.5 %collective-permute-start.7 = (bf16[112,512]{1,0:T(8,128)(2,1)S(1)}, bf16[112,512]{1,0:T(8,128)(2,1)S(1)}, u32[]{:S(2)}, u32[]{:S(2)}) collective-permute-start(bf16[112,512]{1,0:T(8,128)(2,1)S(1)} %bitcast.29), channel_id=1, source_target_pairs={{0,6},{1,7},{2,4},{3,5},{4,2},{5,3},{6,0},{7,1},{8,14},{9,15},{10,... | collective-permute-start | bytes 344072 | tf_op jit(solution)/shard_map/ppermute | solution.py:184
  8.2 0.4 %collective-permute-start.6 = (bf16[112,512]{1,0:T(8,128)(2,1)S(1)}, bf16[112,512]{1,0:T(8,128)(2,1)S(1)}, u32[]{:S(2)}, u32[]{:S(2)}) collective-permute-start(bf16[112,512]{1,0:T(8,128)(2,1)S(1)} %bitcast.30), channel_id=1, source_target_pairs={{0,4},{1,5},{2,6},{3,7},{4,0},{5,1},{6,2},{7,3},{8,12},{9,13},{10,... | collective-permute-start | bytes 344072 | tf_op jit(solution)/shard_map/ppermute | solution.py:184
  8.7 0.5 %collective-permute-start.5 = (bf16[112,512]{1,0:T(8,128)(2,1)S(1)}, bf16[112,512]{1,0:T(8,128)(2,1)S(1)}, u32[]{:S(2)}, u32[]{:S(2)}) collective-permute-start(bf16[112,512]{1,0:T(8,128)(2,1)S(1)} %bitcast.31), channel_id=1, source_target_pairs={{0,2},{1,3},{2,0},{3,1},{4,6},{5,7},{6,4},{7,5},{8,10},{9,11},{10,... | collective-permute-start | bytes 344072 | tf_op jit(solution)/shard_map/ppermute | solution.py:184
  9.2 2.8 %collective-permute-done.refs_1_ = bf16[112,512]{1,0:T(8,128)(2,1)S(1)} collective-permute-done((bf16[112,512]{1,0:T(8,128)(2,1)S(1)}, bf16[112,512]{1,0:T(8,128)(2,1)S(1)}, u32[]{:S(2)}, u32[]{:S(2)}) %collective-permute-start) | collective-permute-done | bytes 114720 | tf_op jit(solution)/shard_map/ppermute | solution.py:184
  12.0 1.7 %collective-permute-start.3 = (bf16[112,512]{1,0:T(8,128)(2,1)S(1)}, bf16[112,512]{1,0:T(8,128)(2,1)S(1)}, u32[]{:S(2)}, u32[]{:S(2)}) collective-permute-start(bf16[112,512]{1,0:T(8,128)(2,1)S(1)} %collective-permute-done.refs_1_), channel_id=1, source_target_pairs={{0,6},{1,7},{2,4},{3,5},{4,2},{5,3},{6,0},{7,1},{8,14},{9,15},{10,... | collective-permute-start | bytes 344072 | tf_op jit(solution)/shard_map/ppermute | solution.py:184
  13.7 1.4 %collective-permute-start.2 = (bf16[112,512]{1,0:T(8,128)(2,1)S(1)}, bf16[112,512]{1,0:T(8,128)(2,1)S(1)}, u32[]{:S(2)}, u32[]{:S(2)}) collective-permute-start(bf16[112,512]{1,0:T(8,128)(2,1)S(1)} %collective-permute-done.refs_1_), channel_id=1, source_target_pairs={{0,4},{1,5},{2,6},{3,7},{4,0},{5,1},{6,2},{7,3},{8,12},{9,13},{10,... | collective-permute-start | bytes 344072 | tf_op jit(solution)/shard_map/ppermute | solution.py:184
  15.1 0.4 %collective-permute-start.1 = (bf16[112,512]{1,0:T(8,128)(2,1)S(1)}, bf16[112,512]{1,0:T(8,128)(2,1)S(1)}, u32[]{:S(2)}, u32[]{:S(2)}) collective-permute-start(bf16[112,512]{1,0:T(8,128)(2,1)S(1)} %collective-permute-done.refs_1_), channel_id=1, source_target_pairs={{0,2},{1,3},{2,0},{3,1},{4,6},{5,7},{6,4},{7,5},{8,10},{9,11},{10,... | collective-permute-start | bytes 344072 | tf_op jit(solution)/shard_map/ppermute | solution.py:184
  15.5 0.5 %collective-permute-done.6.refs_2_ = bf16[112,512]{1,0:T(8,128)(2,1)S(1)} collective-permute-done((bf16[112,512]{1,0:T(8,128)(2,1)S(1)}, bf16[112,512]{1,0:T(8,128)(2,1)S(1)}, u32[]{:S(2)}, u32[]{:S(2)}) %collective-permute-start.6) | collective-permute-done | bytes 114720 | tf_op jit(solution)/shard_map/ppermute | solution.py:184
  16.0 0.5 %collective-permute-start.10 = (bf16[112,512]{1,0:T(8,128)(2,1)S(1)}, bf16[112,512]{1,0:T(8,128)(2,1)S(1)}, u32[]{:S(2)}, u32[]{:S(2)}) collective-permute-start(bf16[112,512]{1,0:T(8,128)(2,1)S(1)} %collective-permute-done.7.refs_3_), channel_id=1, source_target_pairs={{0,1},{1,0},{2,3},{3,2},{4,5},{5,4},{6,7},{7,6},{8,9},{9,8},{10,11... | collective-permute-start | bytes 344072 | tf_op jit(solution)/shard_map/ppermute | solution.py:184
  16.5 1.4 %copy-done = bf16[1,32,7,7,512]{4,1,3,2,0:T(8,128)(2,1)S(1)} copy-done((bf16[1,32,7,7,512]{4,1,3,2,0:T(8,128)(2,1)S(1)}, bf16[1,32,7,7,512]{4,1,3,2,0:T(8,128)(2,1)}, u32[]{:S(2)}) %copy-start) | copy-done | bytes 1605656
  17.9 1.4 %copy-done.2 = bf16[1,32,7,7,512]{4,1,3,2,0:T(8,128)(2,1)S(1)} copy-done((bf16[1,32,7,7,512]{4,1,3,2,0:T(8,128)(2,1)S(1)}, bf16[1,32,7,7,512]{4,1,3,2,0:T(8,128)(2,1)}, u32[]{:S(2)}) %copy-start.2) | copy-done | bytes 1605656
  19.3 1.6 %chunk_scores.3.refs_0_ = f32[16,128]{1,0:T(8,128)S(1)} custom-call(s32[1]{0:T(128)} %bitcast.me_ref, bf16[112,512]{1,0:T(8,128)(2,1)S(1)} %bitcast.32, bf16[112,512]{1,0:T(8,128)(2,1)S(1)} %collective-permute-done.5.refs_1_, bf16[112,512]{1,0:T(8,128)(2,1)S(1)} %collective-permute-done.6.refs_2_, bf16[112,512]{1,0:T(8,128)(2,1)S(1)} %collective-permute-done.7.refs_3_, ...), custom_call_target="tpu_custom_call" | custom-call | flops 1027604480 | tf_op jit(solution)/shard_map/chunk_scores/pallas_call | solution.py:162
  21.0 0.5 %collective-permute-start.13 = (bf16[112,512]{1,0:T(8,128)(2,1)S(1)}, bf16[112,512]{1,0:T(8,128)(2,1)S(1)}, u32[]{:S(2)}, u32[]{:S(2)}) collective-permute-start(bf16[112,512]{1,0:T(8,128)(2,1)S(1)} %collective-permute-done.2.refs_3_), channel_id=1, source_target_pairs={{0,1},{1,0},{2,3},{3,2},{4,5},{5,4},{6,7},{7,6},{8,9},{9,8},{10,11... | collective-permute-start | bytes 344072 | tf_op jit(solution)/shard_map/ppermute | solution.py:184
  21.6 0.4 %collective-permute-start.8 = (bf16[112,512]{1,0:T(8,128)(2,1)S(1)}, bf16[112,512]{1,0:T(8,128)(2,1)S(1)}, u32[]{:S(2)}, u32[]{:S(2)}) collective-permute-start(bf16[112,512]{1,0:T(8,128)(2,1)S(1)} %collective-permute-done.5.refs_1_), channel_id=1, source_target_pairs={{0,1},{1,0},{2,3},{3,2},{4,5},{5,4},{6,7},{7,6},{8,9},{9,8},{10,11... | collective-permute-start | bytes 344072 | tf_op jit(solution)/shard_map/ppermute | solution.py:184
  22.1 0.1 collective-permute-start.14
  22.8 1.2 %chunk_scores.4.refs_0_ = f32[16,128]{1,0:T(8,128)S(1)} custom-call(s32[1]{0:T(128)} %bitcast.me_ref, f32[16,128]{1,0:T(8,128)S(1)} %chunk_scores.3.refs_0_, bf16[112,512]{1,0:T(8,128)(2,1)S(1)} %collective-permute-done.refs_1_, bf16[112,512]{1,0:T(8,128)(2,1)S(1)} %collective-permute-done.1.refs_2_, bf16[112,512]{1,0:T(8,128)(2,1)S(1)} %collective-permute-done.2.refs_3_, ...), custom_call_target="tpu_custom_call" | custom-call | flops 822083584 | tf_op jit(solution)/shard_map/chunk_scores/pallas_call | solution.py:162
  24.1 2.6 %chunk_scores.5 = (f32[16,128]{1,0:T(8,128)S(1)}, f32[16,16]{1,0:T(8,128)}) custom-call(s32[1]{0:T(128)} %bitcast.me_ref, f32[16,128]{1,0:T(8,128)S(1)} %chunk_scores.4.refs_0_, f32[1]{0:T(128)S(6)} %copy.9.refs_1_, s32[1,32]{1,0:T(1,128)S(1)} %bitcast.33, bf16[112,512]{1,0:T(8,128)(2,1)S(1)} %collective-permute-done.8.refs_3_, ...), custom_call_target="tpu_custom_call" | custom-call | flops 1438646272 | tf_op jit(solution)/shard_map/chunk_scores/pallas_call | solution.py:162
  26.8 5.4 %all-to-all-start = ((f32[16,1,16]{2,1,0:T(1,128)}), f32[16,1,16]{2,1,0:T(1,128)S(1)}, u32[]{:S(2)}, u32[]{:S(2)}) async-start(f32[16,1,16]{2,1,0:T(1,128)} %bitcast.13), calls=%async_computation | async-start | bytes 16384 | tf_op jit(solution)/shard_map/all_to_all | solution.py:239
  32.2 0.6 %slice_bitcast_fusion = f32[32,16]{0,1:T(8,128)} fusion(f32[16,128]{1,0:T(8,128)S(1)} %get-tuple-element.16), kind=kLoop, calls=%fused_computation.4 | loop fusion | bytes 4096 | tf_op jit(solution)/shard_map/transpose | solution.py:240
  32.8 5.8 %all-to-all-done = f32[16,1,16]{2,1,0:T(1,128)S(1)} async-done(((f32[16,1,16]{2,1,0:T(1,128)}), f32[16,1,16]{2,1,0:T(1,128)S(1)}, u32[]{:S(2)}, u32[]{:S(2)}) %all-to-all-start) | async-done | bytes 1056 | tf_op jit(solution)/shard_map/all_to_all | solution.py:239
  38.6 0.5 %reduce_sum.9 = f32[16]{0:T(128)} reduce(f32[16,1,16]{2,1,0:T(1,128)S(1)} %all-to-all-done, f32[]{:T(128)} %constant.8.clone.1), dimensions={0,1}, to_apply=%region_0.1 | reduce | flops 240 | bytes 1092 | tf_op jit(solution)/shard_map/reduce_sum | solution.py:240
  (24 shorter events, 0.2 us)
Async XLA Ops:
  1.5 4.2 %collective-permute-start.4 = (bf16[112,512]{1,0:T(8,128)(2,1)S(1)}, bf16[112,512]{1,0:T(8,128)(2,1)S(1)}, u32[]{:S(2)}, u32[]{:S(2)}) collective-permute-start(bf16[112,512]{1,0:T(8,128)(2,1)S(1)} %bitcast.27), channel_id=1, source_target_pairs={{0,1},{1,0},{2,3},{3,2},{4,5},{5,4},{6,7},{7,6},{8,9},{9,8},{10,11... | collective-permute-start | bytes 344072 | tf_op jit(solution)/shard_map/ppermute | solution.py:184
  2.0 10.0 %collective-permute-start = (bf16[112,512]{1,0:T(8,128)(2,1)S(1)}, bf16[112,512]{1,0:T(8,128)(2,1)S(1)}, u32[]{:S(2)}, u32[]{:S(2)}) collective-permute-start(bf16[112,512]{1,0:T(8,128)(2,1)S(1)} %bitcast.28), channel_id=1, source_target_pairs={{0,8},{1,9},{2,10},{3,11},{4,12},{5,13},{6,14},{7,15},{8,0},{9,1},... | collective-permute-start | bytes 344072 | tf_op jit(solution)/shard_map/ppermute | solution.py:184
  5.7 9.3 %collective-permute-start.7 = (bf16[112,512]{1,0:T(8,128)(2,1)S(1)}, bf16[112,512]{1,0:T(8,128)(2,1)S(1)}, u32[]{:S(2)}, u32[]{:S(2)}) collective-permute-start(bf16[112,512]{1,0:T(8,128)(2,1)S(1)} %bitcast.29), channel_id=1, source_target_pairs={{0,6},{1,7},{2,4},{3,5},{4,2},{5,3},{6,0},{7,1},{8,14},{9,15},{10,... | collective-permute-start | bytes 344072 | tf_op jit(solution)/shard_map/ppermute | solution.py:184
  8.2 7.7 %collective-permute-start.6 = (bf16[112,512]{1,0:T(8,128)(2,1)S(1)}, bf16[112,512]{1,0:T(8,128)(2,1)S(1)}, u32[]{:S(2)}, u32[]{:S(2)}) collective-permute-start(bf16[112,512]{1,0:T(8,128)(2,1)S(1)} %bitcast.30), channel_id=1, source_target_pairs={{0,4},{1,5},{2,6},{3,7},{4,0},{5,1},{6,2},{7,3},{8,12},{9,13},{10,... | collective-permute-start | bytes 344072 | tf_op jit(solution)/shard_map/ppermute | solution.py:184
  8.7 7.3 %collective-permute-start.5 = (bf16[112,512]{1,0:T(8,128)(2,1)S(1)}, bf16[112,512]{1,0:T(8,128)(2,1)S(1)}, u32[]{:S(2)}, u32[]{:S(2)}) collective-permute-start(bf16[112,512]{1,0:T(8,128)(2,1)S(1)} %bitcast.31), channel_id=1, source_target_pairs={{0,2},{1,3},{2,0},{3,1},{4,6},{5,7},{6,4},{7,5},{8,10},{9,11},{10,... | collective-permute-start | bytes 344072 | tf_op jit(solution)/shard_map/ppermute | solution.py:184
  12.0 8.9 %collective-permute-start.3 = (bf16[112,512]{1,0:T(8,128)(2,1)S(1)}, bf16[112,512]{1,0:T(8,128)(2,1)S(1)}, u32[]{:S(2)}, u32[]{:S(2)}) collective-permute-start(bf16[112,512]{1,0:T(8,128)(2,1)S(1)} %collective-permute-done.refs_1_), channel_id=1, source_target_pairs={{0,6},{1,7},{2,4},{3,5},{4,2},{5,3},{6,0},{7,1},{8,14},{9,15},{10,... | collective-permute-start | bytes 344072 | tf_op jit(solution)/shard_map/ppermute | solution.py:184
  13.7 7.3 %collective-permute-start.2 = (bf16[112,512]{1,0:T(8,128)(2,1)S(1)}, bf16[112,512]{1,0:T(8,128)(2,1)S(1)}, u32[]{:S(2)}, u32[]{:S(2)}) collective-permute-start(bf16[112,512]{1,0:T(8,128)(2,1)S(1)} %collective-permute-done.refs_1_), channel_id=1, source_target_pairs={{0,4},{1,5},{2,6},{3,7},{4,0},{5,1},{6,2},{7,3},{8,12},{9,13},{10,... | collective-permute-start | bytes 344072 | tf_op jit(solution)/shard_map/ppermute | solution.py:184
  15.1 5.9 %collective-permute-start.1 = (bf16[112,512]{1,0:T(8,128)(2,1)S(1)}, bf16[112,512]{1,0:T(8,128)(2,1)S(1)}, u32[]{:S(2)}, u32[]{:S(2)}) collective-permute-start(bf16[112,512]{1,0:T(8,128)(2,1)S(1)} %collective-permute-done.refs_1_), channel_id=1, source_target_pairs={{0,2},{1,3},{2,0},{3,1},{4,6},{5,7},{6,4},{7,5},{8,10},{9,11},{10,... | collective-permute-start | bytes 344072 | tf_op jit(solution)/shard_map/ppermute | solution.py:184
  16.0 5.6 %collective-permute-start.11 = (bf16[112,512]{1,0:T(8,128)(2,1)S(1)}, bf16[112,512]{1,0:T(8,128)(2,1)S(1)}, u32[]{:S(2)}, u32[]{:S(2)}) collective-permute-start(bf16[112,512]{1,0:T(8,128)(2,1)S(1)} %collective-permute-done.refs_1_), channel_id=1, source_target_pairs={{0,1},{1,0},{2,3},{3,2},{4,5},{5,4},{6,7},{7,6},{8,9},{9,8},{10,11... | collective-permute-start | bytes 344072 | tf_op jit(solution)/shard_map/ppermute | solution.py:184
  16.0 6.1 %collective-permute-start.10 = (bf16[112,512]{1,0:T(8,128)(2,1)S(1)}, bf16[112,512]{1,0:T(8,128)(2,1)S(1)}, u32[]{:S(2)}, u32[]{:S(2)}) collective-permute-start(bf16[112,512]{1,0:T(8,128)(2,1)S(1)} %collective-permute-done.7.refs_3_), channel_id=1, source_target_pairs={{0,1},{1,0},{2,3},{3,2},{4,5},{5,4},{6,7},{7,6},{8,9},{9,8},{10,11... | collective-permute-start | bytes 344072 | tf_op jit(solution)/shard_map/ppermute | solution.py:184
  16.5 1.4 %copy-start = (bf16[1,32,7,7,512]{4,1,3,2,0:T(8,128)(2,1)S(1)}, bf16[1,32,7,7,512]{4,1,3,2,0:T(8,128)(2,1)}, u32[]{:S(2)}) copy-start(bf16[1,32,7,7,512]{4,1,3,2,0:T(8,128)(2,1)} %param.6) | copy-start | bytes 4816900
  17.9 1.4 %copy-start.2 = (bf16[1,32,7,7,512]{4,1,3,2,0:T(8,128)(2,1)S(1)}, bf16[1,32,7,7,512]{4,1,3,2,0:T(8,128)(2,1)}, u32[]{:S(2)}) copy-start(bf16[1,32,7,7,512]{4,1,3,2,0:T(8,128)(2,1)} %param.7) | copy-start | bytes 4816900
  19.3 3.5 %copy-start.1 = (bf16[1,32,7,7,512]{4,1,3,2,0:T(8,128)(2,1)S(1)}, bf16[1,32,7,7,512]{4,1,3,2,0:T(8,128)(2,1)}, u32[]{:S(2)}) copy-start(bf16[1,32,7,7,512]{4,1,3,2,0:T(8,128)(2,1)} %param.6) | copy-start | bytes 4816900
  19.3 3.5 %copy-start.3 = (bf16[1,32,7,7,512]{4,1,3,2,0:T(8,128)(2,1)S(1)}, bf16[1,32,7,7,512]{4,1,3,2,0:T(8,128)(2,1)}, u32[]{:S(2)}) copy-start(bf16[1,32,7,7,512]{4,1,3,2,0:T(8,128)(2,1)} %param.7) | copy-start | bytes 4816900
  21.0 3.1 %collective-permute-start.12 = (bf16[112,512]{1,0:T(8,128)(2,1)S(1)}, bf16[112,512]{1,0:T(8,128)(2,1)S(1)}, u32[]{:S(2)}, u32[]{:S(2)}) collective-permute-start(bf16[112,512]{1,0:T(8,128)(2,1)S(1)} %collective-permute-done.1.refs_2_), channel_id=1, source_target_pairs={{0,1},{1,0},{2,3},{3,2},{4,5},{5,4},{6,7},{7,6},{8,9},{9,8},{10,11... | collective-permute-start | bytes 344072 | tf_op jit(solution)/shard_map/ppermute | solution.py:184
  21.0 3.1 %collective-permute-start.13 = (bf16[112,512]{1,0:T(8,128)(2,1)S(1)}, bf16[112,512]{1,0:T(8,128)(2,1)S(1)}, u32[]{:S(2)}, u32[]{:S(2)}) collective-permute-start(bf16[112,512]{1,0:T(8,128)(2,1)S(1)} %collective-permute-done.2.refs_3_), channel_id=1, source_target_pairs={{0,1},{1,0},{2,3},{3,2},{4,5},{5,4},{6,7},{7,6},{8,9},{9,8},{10,11... | collective-permute-start | bytes 344072 | tf_op jit(solution)/shard_map/ppermute | solution.py:184
  21.5 2.5 %collective-permute-start.9 = (bf16[112,512]{1,0:T(8,128)(2,1)S(1)}, bf16[112,512]{1,0:T(8,128)(2,1)S(1)}, u32[]{:S(2)}, u32[]{:S(2)}) collective-permute-start(bf16[112,512]{1,0:T(8,128)(2,1)S(1)} %collective-permute-done.6.refs_2_), channel_id=1, source_target_pairs={{0,1},{1,0},{2,3},{3,2},{4,5},{5,4},{6,7},{7,6},{8,9},{9,8},{10,11... | collective-permute-start | bytes 344072 | tf_op jit(solution)/shard_map/ppermute | solution.py:184
  21.6 2.5 %collective-permute-start.8 = (bf16[112,512]{1,0:T(8,128)(2,1)S(1)}, bf16[112,512]{1,0:T(8,128)(2,1)S(1)}, u32[]{:S(2)}, u32[]{:S(2)}) collective-permute-start(bf16[112,512]{1,0:T(8,128)(2,1)S(1)} %collective-permute-done.5.refs_1_), channel_id=1, source_target_pairs={{0,1},{1,0},{2,3},{3,2},{4,5},{5,4},{6,7},{7,6},{8,9},{9,8},{10,11... | collective-permute-start | bytes 344072 | tf_op jit(solution)/shard_map/ppermute | solution.py:184
  22.1 2.1 %collective-permute-start.14 = (bf16[112,512]{1,0:T(8,128)(2,1)S(1)}, bf16[112,512]{1,0:T(8,128)(2,1)S(1)}, u32[]{:S(2)}, u32[]{:S(2)}) collective-permute-start(bf16[112,512]{1,0:T(8,128)(2,1)S(1)} %collective-permute-done.3.refs_4_), channel_id=1, source_target_pairs={{0,1},{1,0},{2,3},{3,2},{4,5},{5,4},{6,7},{7,6},{8,9},{9,8},{10,11... | collective-permute-start | bytes 344072 | tf_op jit(solution)/shard_map/ppermute | solution.py:184
  22.8 1.3 %copy-start.4 = (s32[32,1]{0,1:T(1,128)S(1)}, s32[32,1]{0,1:T(1,128)}, u32[]{:S(2)}) copy-start(s32[32,1]{0,1:T(1,128)} %param.11) | copy-start | bytes 388
  26.8 11.8 %all-to-all-start = ((f32[16,1,16]{2,1,0:T(1,128)}), f32[16,1,16]{2,1,0:T(1,128)S(1)}, u32[]{:S(2)}, u32[]{:S(2)}) async-start(f32[16,1,16]{2,1,0:T(1,128)} %bitcast.13), calls=%async_computation | async-start | bytes 16384 | tf_op jit(solution)/shard_map/all_to_all | solution.py:239

commit v4 on v3

--- a/solution.py
+++ b/solution.py
@@ -221,20 +221,23 @@
     scores, came, sent_on = None, {1: other}, {}
     for k in range(len(groups) + 1):
         last, group = k == len(groups), groups[k] if k < len(groups) else []
-        if k != 1 or len(groups) > 2:
-            came, sent_on = came | sent_on, {}
+        came, sent_on = came | sent_on, {}
         distances, arrays = group + list(came), [held[d] for d in group] + list(came.values())
         late = group[1:] if k else []
         if late:
             *sent, scores = lax.optimization_barrier((*[held[d] for d in late], scores))
         sent = dict(zip(late, sent)) if late else {}
         came = {}
-        sent_on |= {d ^ 1: across(sent.get(d, held[d]), 1) for d in group if d}
+        if k:
+            sent_on = {d ^ 1: across(sent.get(d, held[d]), 1) for d in group}
         places = [(test, 0) for test in range(len(arrays))]
         done = chunk_scores(
             distances, places, last, side, size, scale, me, ckpt_weights, ids, scores, arrays, act, grad
         )
         scores = done[0]
+        if k == 0:
+            *sent, scores = lax.optimization_barrier((*[held[d] for d in group[1:]], scores))
+            sent_on = {d ^ 1: across(x, 1) for d, x in zip(group[1:], sent)}
     scores, packed = done
     received = lax.all_to_all(packed, "rows", split_axis=0, concat_axis=0, tiled=True)
     return scores[:, :tr_dev].T, jnp.sum(received, axis=0, keepdims=True)

time: 39.4 us -> 40 us (1.015)
  transfers between devices with their start and end apart: 16 -> 16, of which waited for: 3 -> 3; matrix products, arithmetic and copies ran while one was open for 2% -> 2% of each run, Pallas kernels for 7% -> 9%
where the time goes in v4:
time: 40 us; the launch traced here: 39.8 us
  starting transfers between devices  18.3 us (46%)
  waiting for transfers between devices  9.36 us (23%)
  Pallas kernels  5.81 us (15%)
  local copies, waits for them, and re-layouts  3.45 us (9%)
  other arithmetic  1.43 us (4%)
  between operations  1.39 us (3%)
    ppermute x15, starting transfers between devices, across(): return lax.ppermute(x, 'rows', [(i, i ^ distance) for i in range(size)])  12.9 us
    pallas_call x3, Pallas kernels, chunk_scores(): pl.pallas_call(functools.partial(chunk_kernel, distances, places, first,...  5.81 us
    all_to_all x1, waiting for transfers between devices, body(): lax.all_to_all(packed, 'rows', split_axis=0, concat_axis=0, tiled=True)  5.8 us
    all_to_all x1, starting transfers between devices, body(): lax.all_to_all(packed, 'rows', split_axis=0, concat_axis=0, tiled=True)  5.42 us
    ppermute x15, waiting for transfers between devices, across(): return lax.ppermute(x, 'rows', [(i, i ^ distance) for i in range(size)])  3.56 us
    unnamed x10, local copies, waits for them, and re-layouts  2.85 us
    another operation x1, other arithmetic, pack_test(): maps = jnp.stack([act, grad])  0.89 us
  transfers between devices with their start and end apart: 16, of which 3 were waited for; matrix products, arithmetic and copies ran while one was open for 2% of the time, Pallas kernels for 9%

profile of v4, /device:TPU:0, one launch (start us, length us, event | category | flops | bytes accessed | tf_op | source)
XLA Modules:
  0.0 39.8 jit_solution(4469222877679191935)
XLA Ops:
  0.6 0.9 %fusion.2 = bf16[2,7,8,512]{3,2,1,0:T(8,128)(2,1)S(1)} fusion(bf16[1,7,7,512]{3,2,1,0:T(8,128)(2,1)} %bitcast.34, bf16[1,7,7,512]{3,2,1,0:T(8,128)(2,1)} %bitcast.35), kind=kLoop, calls=%fused_computation.3 | loop fusion | flops 401408 | bytes 215040 | tf_op jit(solution)/shard_map/stack | solution.py:22
  1.5 0.5 %collective-permute-start.4 = (bf16[112,512]{1,0:T(8,128)(2,1)S(1)}, bf16[112,512]{1,0:T(8,128)(2,1)S(1)}, u32[]{:S(2)}, u32[]{:S(2)}) collective-permute-start(bf16[112,512]{1,0:T(8,128)(2,1)S(1)} %bitcast.27), channel_id=1, source_target_pairs={{0,1},{1,0},{2,3},{3,2},{4,5},{5,4},{6,7},{7,6},{8,9},{9,8},{10,11... | collective-permute-start | bytes 344072 | tf_op jit(solution)/shard_map/ppermute | solution.py:184
  2.0 3.7 %collective-permute-start = (bf16[112,512]{1,0:T(8,128)(2,1)S(1)}, bf16[112,512]{1,0:T(8,128)(2,1)S(1)}, u32[]{:S(2)}, u32[]{:S(2)}) collective-permute-start(bf16[112,512]{1,0:T(8,128)(2,1)S(1)} %bitcast.28), channel_id=1, source_target_pairs={{0,8},{1,9},{2,10},{3,11},{4,12},{5,13},{6,14},{7,15},{8,0},{9,1},... | collective-permute-start | bytes 344072 | tf_op jit(solution)/shard_map/ppermute | solution.py:184
  5.7 1.5 %collective-permute-start.5 = (bf16[112,512]{1,0:T(8,128)(2,1)S(1)}, bf16[112,512]{1,0:T(8,128)(2,1)S(1)}, u32[]{:S(2)}, u32[]{:S(2)}) collective-permute-start(bf16[112,512]{1,0:T(8,128)(2,1)S(1)} %bitcast.29), channel_id=1, source_target_pairs={{0,2},{1,3},{2,0},{3,1},{4,6},{5,7},{6,4},{7,5},{8,10},{9,11},{10,... | collective-permute-start | bytes 344072 | tf_op jit(solution)/shard_map/ppermute | solution.py:184
  7.2 1.6 %collective-permute-start.6 = (bf16[112,512]{1,0:T(8,128)(2,1)S(1)}, bf16[112,512]{1,0:T(8,128)(2,1)S(1)}, u32[]{:S(2)}, u32[]{:S(2)}) collective-permute-start(bf16[112,512]{1,0:T(8,128)(2,1)S(1)} %bitcast.30), channel_id=1, source_target_pairs={{0,4},{1,5},{2,6},{3,7},{4,0},{5,1},{6,2},{7,3},{8,12},{9,13},{10,... | collective-permute-start | bytes 344072 | tf_op jit(solution)/shard_map/ppermute | solution.py:184
  8.8 0.4 collective-permute-start.7
  9.2 2.8 %collective-permute-done.refs_1_ = bf16[112,512]{1,0:T(8,128)(2,1)S(1)} collective-permute-done((bf16[112,512]{1,0:T(8,128)(2,1)S(1)}, bf16[112,512]{1,0:T(8,128)(2,1)S(1)}, u32[]{:S(2)}, u32[]{:S(2)}) %collective-permute-start) | collective-permute-done | bytes 114720 | tf_op jit(solution)/shard_map/ppermute | solution.py:184
  12.0 1.6 %collective-permute-start.1 = (bf16[112,512]{1,0:T(8,128)(2,1)S(1)}, bf16[112,512]{1,0:T(8,128)(2,1)S(1)}, u32[]{:S(2)}, u32[]{:S(2)}) collective-permute-start(bf16[112,512]{1,0:T(8,128)(2,1)S(1)} %collective-permute-done.refs_1_), channel_id=1, source_target_pairs={{0,2},{1,3},{2,0},{3,1},{4,6},{5,7},{6,4},{7,5},{8,10},{9,11},{10,... | collective-permute-start | bytes 344072 | tf_op jit(solution)/shard_map/ppermute | solution.py:184
  13.6 0.6 %collective-permute-start.2 = (bf16[112,512]{1,0:T(8,128)(2,1)S(1)}, bf16[112,512]{1,0:T(8,128)(2,1)S(1)}, u32[]{:S(2)}, u32[]{:S(2)}) collective-permute-start(bf16[112,512]{1,0:T(8,128)(2,1)S(1)} %collective-permute-done.refs_1_), channel_id=1, source_target_pairs={{0,4},{1,5},{2,6},{3,7},{4,0},{5,1},{6,2},{7,3},{8,12},{9,13},{10,... | collective-permute-start | bytes 344072 | tf_op jit(solution)/shard_map/ppermute | solution.py:184
  14.2 1.3 %collective-permute-start.3 = (bf16[112,512]{1,0:T(8,128)(2,1)S(1)}, bf16[112,512]{1,0:T(8,128)(2,1)S(1)}, u32[]{:S(2)}, u32[]{:S(2)}) collective-permute-start(bf16[112,512]{1,0:T(8,128)(2,1)S(1)} %collective-permute-done.refs_1_), channel_id=1, source_target_pairs={{0,6},{1,7},{2,4},{3,5},{4,2},{5,3},{6,0},{7,1},{8,14},{9,15},{10,... | collective-permute-start | bytes 344072 | tf_op jit(solution)/shard_map/ppermute | solution.py:184
  15.5 0.7 %collective-permute-done.7.refs_3_ = bf16[112,512]{1,0:T(8,128)(2,1)S(1)} collective-permute-done((bf16[112,512]{1,0:T(8,128)(2,1)S(1)}, bf16[112,512]{1,0:T(8,128)(2,1)S(1)}, u32[]{:S(2)}, u32[]{:S(2)}) %collective-permute-start.7) | collective-permute-done | bytes 114720 | tf_op jit(solution)/shard_map/ppermute | solution.py:184
  16.2 1.4 %copy-done = bf16[1,32,7,7,512]{4,1,3,2,0:T(8,128)(2,1)S(1)} copy-done((bf16[1,32,7,7,512]{4,1,3,2,0:T(8,128)(2,1)S(1)}, bf16[1,32,7,7,512]{4,1,3,2,0:T(8,128)(2,1)}, u32[]{:S(2)}) %copy-start) | copy-done | bytes 1605656
  17.6 1.4 %copy-done.2 = bf16[1,32,7,7,512]{4,1,3,2,0:T(8,128)(2,1)S(1)} copy-done((bf16[1,32,7,7,512]{4,1,3,2,0:T(8,128)(2,1)S(1)}, bf16[1,32,7,7,512]{4,1,3,2,0:T(8,128)(2,1)}, u32[]{:S(2)}) %copy-start.2) | copy-done | bytes 1605656
  19.1 1.6 %chunk_scores.3.refs_0_ = f32[16,128]{1,0:T(8,128)S(1)} custom-call(s32[1]{0:T(128)} %bitcast.me_ref, bf16[112,512]{1,0:T(8,128)(2,1)S(1)} %bitcast.32, bf16[112,512]{1,0:T(8,128)(2,1)S(1)} %collective-permute-done.5.refs_1_, bf16[112,512]{1,0:T(8,128)(2,1)S(1)} %collective-permute-done.6.refs_2_, bf16[112,512]{1,0:T(8,128)(2,1)S(1)} %collective-permute-done.7.refs_3_, ...), custom_call_target="tpu_custom_call" | custom-call | flops 1027604480 | tf_op jit(solution)/shard_map/chunk_scores/pallas_call | solution.py:162
  20.7 0.5 %collective-permute-start.8 = (bf16[112,512]{1,0:T(8,128)(2,1)S(1)}, bf16[112,512]{1,0:T(8,128)(2,1)S(1)}, u32[]{:S(2)}, u32[]{:S(2)}) collective-permute-start(bf16[112,512]{1,0:T(8,128)(2,1)S(1)} %collective-permute-done.5.refs_1_), channel_id=1, source_target_pairs={{0,1},{1,0},{2,3},{3,2},{4,5},{5,4},{6,7},{7,6},{8,9},{9,8},{10,11... | collective-permute-start | bytes 344072 | tf_op jit(solution)/shard_map/ppermute | solution.py:184
  22.0 0.5 %collective-permute-start.11 = (bf16[112,512]{1,0:T(8,128)(2,1)S(1)}, bf16[112,512]{1,0:T(8,128)(2,1)S(1)}, u32[]{:S(2)}, u32[]{:S(2)}) collective-permute-start(bf16[112,512]{1,0:T(8,128)(2,1)S(1)} %collective-permute-done.refs_1_), channel_id=1, source_target_pairs={{0,1},{1,0},{2,3},{3,2},{4,5},{5,4},{6,7},{7,6},{8,9},{9,8},{10,11... | collective-permute-start | bytes 344072 | tf_op jit(solution)/shard_map/ppermute | solution.py:184
  22.5 0.1 collective-permute-start.12
  22.6 0.4 %collective-permute-start.13 = (bf16[112,512]{1,0:T(8,128)(2,1)S(1)}, bf16[112,512]{1,0:T(8,128)(2,1)S(1)}, u32[]{:S(2)}, u32[]{:S(2)}) collective-permute-start(bf16[112,512]{1,0:T(8,128)(2,1)S(1)} %collective-permute-done.2.refs_3_), channel_id=1, source_target_pairs={{0,1},{1,0},{2,3},{3,2},{4,5},{5,4},{6,7},{7,6},{8,9},{9,8},{10,11... | collective-permute-start | bytes 344072 | tf_op jit(solution)/shard_map/ppermute | solution.py:184
  23.1 2.1 %chunk_scores.4.refs_0_ = f32[16,128]{1,0:T(8,128)S(1)} custom-call(s32[1]{0:T(128)} %bitcast.me_ref, f32[16,128]{1,0:T(8,128)S(1)} %chunk_scores.3.refs_0_, bf16[112,512]{1,0:T(8,128)(2,1)S(1)} %collective-permute-done.refs_1_, bf16[112,512]{1,0:T(8,128)(2,1)S(1)} %collective-permute-done.1.refs_2_, bf16[112,512]{1,0:T(8,128)(2,1)S(1)} %collective-permute-done.2.refs_3_, ...), custom_call_target="tpu_custom_call" | custom-call | flops 1438646272 | tf_op jit(solution)/shard_map/chunk_scores/pallas_call | solution.py:162
  25.3 2.1 %chunk_scores.5 = (f32[16,128]{1,0:T(8,128)S(1)}, f32[16,16]{1,0:T(8,128)}) custom-call(s32[1]{0:T(128)} %bitcast.me_ref, f32[16,128]{1,0:T(8,128)S(1)} %chunk_scores.4.refs_0_, f32[1]{0:T(128)S(6)} %copy.9.refs_1_, s32[1,32]{1,0:T(1,128)S(1)} %bitcast.33, bf16[112,512]{1,0:T(8,128)(2,1)S(1)} %collective-permute-done.11.refs_3_, ...), custom_call_target="tpu_custom_call" | custom-call | flops 822083584 | tf_op jit(solution)/shard_map/chunk_scores/pallas_call | solution.py:162
  27.4 5.4 %all-to-all-start = ((f32[16,1,16]{2,1,0:T(1,128)}), f32[16,1,16]{2,1,0:T(1,128)S(1)}, u32[]{:S(2)}, u32[]{:S(2)}) async-start(f32[16,1,16]{2,1,0:T(1,128)} %bitcast.13), calls=%async_computation | async-start | bytes 16384 | tf_op jit(solution)/shard_map/all_to_all | solution.py:242
  32.8 0.6 %slice_bitcast_fusion = f32[32,16]{0,1:T(8,128)} fusion(f32[16,128]{1,0:T(8,128)S(1)} %get-tuple-element.24), kind=kLoop, calls=%fused_computation.4 | loop fusion | bytes 4096 | tf_op jit(solution)/shard_map/transpose | solution.py:243
  33.4 5.8 %all-to-all-done = f32[16,1,16]{2,1,0:T(1,128)S(1)} async-done(((f32[16,1,16]{2,1,0:T(1,128)}), f32[16,1,16]{2,1,0:T(1,128)S(1)}, u32[]{:S(2)}, u32[]{:S(2)}) %all-to-all-start) | async-done | bytes 1056 | tf_op jit(solution)/shard_map/all_to_all | solution.py:242
  39.2 0.5 %reduce_sum.9 = f32[16]{0:T(128)} reduce(f32[16,1,16]{2,1,0:T(1,128)S(1)} %all-to-all-done, f32[]{:T(128)} %constant.8.clone.1), dimensions={0,1}, to_apply=%region_0.1 | reduce | flops 240 | bytes 1092 | tf_op jit(solution)/shard_map/reduce_sum | solution.py:243
  (24 shorter events, 0.3 us)
Async XLA Ops:
  1.5 4.2 %collective-permute-start.4 = (bf16[112,512]{1,0:T(8,128)(2,1)S(1)}, bf16[112,512]{1,0:T(8,128)(2,1)S(1)}, u32[]{:S(2)}, u32[]{:S(2)}) collective-permute-start(bf16[112,512]{1,0:T(8,128)(2,1)S(1)} %bitcast.27), channel_id=1, source_target_pairs={{0,1},{1,0},{2,3},{3,2},{4,5},{5,4},{6,7},{7,6},{8,9},{9,8},{10,11... | collective-permute-start | bytes 344072 | tf_op jit(solution)/shard_map/ppermute | solution.py:184
  2.0 10.0 %collective-permute-start = (bf16[112,512]{1,0:T(8,128)(2,1)S(1)}, bf16[112,512]{1,0:T(8,128)(2,1)S(1)}, u32[]{:S(2)}, u32[]{:S(2)}) collective-permute-start(bf16[112,512]{1,0:T(8,128)(2,1)S(1)} %bitcast.28), channel_id=1, source_target_pairs={{0,8},{1,9},{2,10},{3,11},{4,12},{5,13},{6,14},{7,15},{8,0},{9,1},... | collective-permute-start | bytes 344072 | tf_op jit(solution)/shard_map/ppermute | solution.py:184
  5.7 8.5 %collective-permute-start.5 = (bf16[112,512]{1,0:T(8,128)(2,1)S(1)}, bf16[112,512]{1,0:T(8,128)(2,1)S(1)}, u32[]{:S(2)}, u32[]{:S(2)}) collective-permute-start(bf16[112,512]{1,0:T(8,128)(2,1)S(1)} %bitcast.29), channel_id=1, source_target_pairs={{0,2},{1,3},{2,0},{3,1},{4,6},{5,7},{6,4},{7,5},{8,10},{9,11},{10,... | collective-permute-start | bytes 344072 | tf_op jit(solution)/shard_map/ppermute | solution.py:184
  7.2 8.3 %collective-permute-start.6 = (bf16[112,512]{1,0:T(8,128)(2,1)S(1)}, bf16[112,512]{1,0:T(8,128)(2,1)S(1)}, u32[]{:S(2)}, u32[]{:S(2)}) collective-permute-start(bf16[112,512]{1,0:T(8,128)(2,1)S(1)} %bitcast.30), channel_id=1, source_target_pairs={{0,4},{1,5},{2,6},{3,7},{4,0},{5,1},{6,2},{7,3},{8,12},{9,13},{10,... | collective-permute-start | bytes 344072 | tf_op jit(solution)/shard_map/ppermute | solution.py:184
  8.8 7.4 %collective-permute-start.7 = (bf16[112,512]{1,0:T(8,128)(2,1)S(1)}, bf16[112,512]{1,0:T(8,128)(2,1)S(1)}, u32[]{:S(2)}, u32[]{:S(2)}) collective-permute-start(bf16[112,512]{1,0:T(8,128)(2,1)S(1)} %bitcast.31), channel_id=1, source_target_pairs={{0,6},{1,7},{2,4},{3,5},{4,2},{5,3},{6,0},{7,1},{8,14},{9,15},{10,... | collective-permute-start | bytes 344072 | tf_op jit(solution)/shard_map/ppermute | solution.py:184
  12.0 9.2 %collective-permute-start.1 = (bf16[112,512]{1,0:T(8,128)(2,1)S(1)}, bf16[112,512]{1,0:T(8,128)(2,1)S(1)}, u32[]{:S(2)}, u32[]{:S(2)}) collective-permute-start(bf16[112,512]{1,0:T(8,128)(2,1)S(1)} %collective-permute-done.refs_1_), channel_id=1, source_target_pairs={{0,2},{1,3},{2,0},{3,1},{4,6},{5,7},{6,4},{7,5},{8,10},{9,11},{10,... | collective-permute-start | bytes 344072 | tf_op jit(solution)/shard_map/ppermute | solution.py:184
  13.6 8.4 %collective-permute-start.2 = (bf16[112,512]{1,0:T(8,128)(2,1)S(1)}, bf16[112,512]{1,0:T(8,128)(2,1)S(1)}, u32[]{:S(2)}, u32[]{:S(2)}) collective-permute-start(bf16[112,512]{1,0:T(8,128)(2,1)S(1)} %collective-permute-done.refs_1_), channel_id=1, source_target_pairs={{0,4},{1,5},{2,6},{3,7},{4,0},{5,1},{6,2},{7,3},{8,12},{9,13},{10,... | collective-permute-start | bytes 344072 | tf_op jit(solution)/shard_map/ppermute | solution.py:184
  14.2 8.3 %collective-permute-start.3 = (bf16[112,512]{1,0:T(8,128)(2,1)S(1)}, bf16[112,512]{1,0:T(8,128)(2,1)S(1)}, u32[]{:S(2)}, u32[]{:S(2)}) collective-permute-start(bf16[112,512]{1,0:T(8,128)(2,1)S(1)} %collective-permute-done.refs_1_), channel_id=1, source_target_pairs={{0,6},{1,7},{2,4},{3,5},{4,2},{5,3},{6,0},{7,1},{8,14},{9,15},{10,... | collective-permute-start | bytes 344072 | tf_op jit(solution)/shard_map/ppermute | solution.py:184
  16.2 1.4 %copy-start = (bf16[1,32,7,7,512]{4,1,3,2,0:T(8,128)(2,1)S(1)}, bf16[1,32,7,7,512]{4,1,3,2,0:T(8,128)(2,1)}, u32[]{:S(2)}) copy-start(bf16[1,32,7,7,512]{4,1,3,2,0:T(8,128)(2,1)} %param.6) | copy-start | bytes 4816900
  17.6 1.4 %copy-start.2 = (bf16[1,32,7,7,512]{4,1,3,2,0:T(8,128)(2,1)S(1)}, bf16[1,32,7,7,512]{4,1,3,2,0:T(8,128)(2,1)}, u32[]{:S(2)}) copy-start(bf16[1,32,7,7,512]{4,1,3,2,0:T(8,128)(2,1)} %param.7) | copy-start | bytes 4816900
  19.1 4.0 %copy-start.1 = (bf16[1,32,7,7,512]{4,1,3,2,0:T(8,128)(2,1)S(1)}, bf16[1,32,7,7,512]{4,1,3,2,0:T(8,128)(2,1)}, u32[]{:S(2)}) copy-start(bf16[1,32,7,7,512]{4,1,3,2,0:T(8,128)(2,1)} %param.6) | copy-start | bytes 4816900
  19.1 4.0 %copy-start.3 = (bf16[1,32,7,7,512]{4,1,3,2,0:T(8,128)(2,1)S(1)}, bf16[1,32,7,7,512]{4,1,3,2,0:T(8,128)(2,1)}, u32[]{:S(2)}) copy-start(bf16[1,32,7,7,512]{4,1,3,2,0:T(8,128)(2,1)} %param.7) | copy-start | bytes 4816900
  20.6 1.9 %collective-permute-start.10 = (bf16[112,512]{1,0:T(8,128)(2,1)S(1)}, bf16[112,512]{1,0:T(8,128)(2,1)S(1)}, u32[]{:S(2)}, u32[]{:S(2)}) collective-permute-start(bf16[112,512]{1,0:T(8,128)(2,1)S(1)} %collective-permute-done.7.refs_3_), channel_id=1, source_target_pairs={{0,1},{1,0},{2,3},{3,2},{4,5},{5,4},{6,7},{7,6},{8,9},{9,8},{10,11... | collective-permute-start | bytes 344072 | tf_op jit(solution)/shard_map/ppermute | solution.py:184
  20.7 2.3 %collective-permute-start.8 = (bf16[112,512]{1,0:T(8,128)(2,1)S(1)}, bf16[112,512]{1,0:T(8,128)(2,1)S(1)}, u32[]{:S(2)}, u32[]{:S(2)}) collective-permute-start(bf16[112,512]{1,0:T(8,128)(2,1)S(1)} %collective-permute-done.5.refs_1_), channel_id=1, source_target_pairs={{0,1},{1,0},{2,3},{3,2},{4,5},{5,4},{6,7},{7,6},{8,9},{9,8},{10,11... | collective-permute-start | bytes 344072 | tf_op jit(solution)/shard_map/ppermute | solution.py:184
  21.2 1.9 %collective-permute-start.9 = (bf16[112,512]{1,0:T(8,128)(2,1)S(1)}, bf16[112,512]{1,0:T(8,128)(2,1)S(1)}, u32[]{:S(2)}, u32[]{:S(2)}) collective-permute-start(bf16[112,512]{1,0:T(8,128)(2,1)S(1)} %collective-permute-done.6.refs_2_), channel_id=1, source_target_pairs={{0,1},{1,0},{2,3},{3,2},{4,5},{5,4},{6,7},{7,6},{8,9},{9,8},{10,11... | collective-permute-start | bytes 344072 | tf_op jit(solution)/shard_map/ppermute | solution.py:184
  22.0 3.3 %copy-start.4 = (s32[32,1]{0,1:T(1,128)S(1)}, s32[32,1]{0,1:T(1,128)}, u32[]{:S(2)}) copy-start(s32[32,1]{0,1:T(1,128)} %param.11) | copy-start | bytes 388
  22.0 3.2 %collective-permute-start.11 = (bf16[112,512]{1,0:T(8,128)(2,1)S(1)}, bf16[112,512]{1,0:T(8,128)(2,1)S(1)}, u32[]{:S(2)}, u32[]{:S(2)}) collective-permute-start(bf16[112,512]{1,0:T(8,128)(2,1)S(1)} %collective-permute-done.refs_1_), channel_id=1, source_target_pairs={{0,1},{1,0},{2,3},{3,2},{4,5},{5,4},{6,7},{7,6},{8,9},{9,8},{10,11... | collective-permute-start | bytes 344072 | tf_op jit(solution)/shard_map/ppermute | solution.py:184
  22.5 2.7 %collective-permute-start.12 = (bf16[112,512]{1,0:T(8,128)(2,1)S(1)}, bf16[112,512]{1,0:T(8,128)(2,1)S(1)}, u32[]{:S(2)}, u32[]{:S(2)}) collective-permute-start(bf16[112,512]{1,0:T(8,128)(2,1)S(1)} %collective-permute-done.1.refs_2_), channel_id=1, source_target_pairs={{0,1},{1,0},{2,3},{3,2},{4,5},{5,4},{6,7},{7,6},{8,9},{9,8},{10,11... | collective-permute-start | bytes 344072 | tf_op jit(solution)/shard_map/ppermute | solution.py:184
  22.6 2.7 %collective-permute-start.13 = (bf16[112,512]{1,0:T(8,128)(2,1)S(1)}, bf16[112,512]{1,0:T(8,128)(2,1)S(1)}, u32[]{:S(2)}, u32[]{:S(2)}) collective-permute-start(bf16[112,512]{1,0:T(8,128)(2,1)S(1)} %collective-permute-done.2.refs_3_), channel_id=1, source_target_pairs={{0,1},{1,0},{2,3},{3,2},{4,5},{5,4},{6,7},{7,6},{8,9},{9,8},{10,11... | collective-permute-start | bytes 344072 | tf_op jit(solution)/shard_map/ppermute | solution.py:184
  23.0 2.2 %collective-permute-start.14 = (bf16[112,512]{1,0:T(8,128)(2,1)S(1)}, bf16[112,512]{1,0:T(8,128)(2,1)S(1)}, u32[]{:S(2)}, u32[]{:S(2)}) collective-permute-start(bf16[112,512]{1,0:T(8,128)(2,1)S(1)} %collective-permute-done.3.refs_4_), channel_id=1, source_target_pairs={{0,1},{1,0},{2,3},{3,2},{4,5},{5,4},{6,7},{7,6},{8,9},{9,8},{10,11... | collective-permute-start | bytes 344072 | tf_op jit(solution)/shard_map/ppermute | solution.py:184
  27.4 11.8 %all-to-all-start = ((f32[16,1,16]{2,1,0:T(1,128)}), f32[16,1,16]{2,1,0:T(1,128)S(1)}, u32[]{:S(2)}, u32[]{:S(2)}) async-start(f32[16,1,16]{2,1,0:T(1,128)} %bitcast.13), calls=%async_computation | async-start | bytes 16384 | tf_op jit(solution)/shard_map/all_to_all | solution.py:242
